TPU v7x, 32 devices: a whole 2x2x4 slice. The times are simulated.
32 devices in a mesh: dp: 2 (over x), seq: 16 (over z, y, core).
Axes of the slice: x: 2, y: 2, z: 4, core: 2. Of those that a mesh axis runs over, the one named last changes fastest.
Arguments:
- queries: bfloat16 [2, 16, 48, 1536], P('dp', 'seq'), may hold values from -100 to 100
- key_field: bfloat16 [2, 16, 48, 1536], P('dp', 'seq'), may hold values from -7 to 7
- value_field: bfloat16 [2, 16, 48, 1536], P('dp', 'seq'), may hold values from -6 to 6
- out_grad: bfloat16 [2, 16, 48, 1536], P('dp', 'seq'), may hold values from -6 to 6
- out_weight: bfloat16 [1536, 1536], P('seq'), may hold values from -0.15625 to 0.15625
- frame_video: int32 [2, 16], P('dp'), may hold values from 0 to 3, never falling along the last dimension, each value on 1 to 8 neighbouring positions
Outputs:
- mixed_out: bfloat16 [2, 16, 48, 1536], P('dp', 'seq')
- query_grad: bfloat16 [2, 16, 48, 1536], P('dp', 'seq')
- key_grad: bfloat16 [2, 16, 48, 1536], P('dp', 'seq')
- value_grad: bfloat16 [2, 16, 48, 1536], P('dp', 'seq')
- weight_grad: float32 [1536, 1536], P('seq')
Inputs may be any that keep to these rules, and one draw needn't show every extreme that they name: `frame_video`: each replica's frames are grouped into whole videos in order: ids never fall, each video has 1 to min(32, 8) frames and one has exactly that many.
All inputs are finite; a program needn't handle non-finite values.
Results may differ from a plain program's by a relative error of at most 0.04.
Values may be sent and summed in bfloat16 or wider, within the bound.
A program may use at most 128 MiB of HBM per device.

v0:
```python
import jax
import jax.numpy as jnp
from jax import lax
from jax.sharding import PartitionSpec as P

HEAD = 128


def attend_forward(query4, key4, value4, allowed, factor):
    logits = (
        jnp.einsum("fphe,gphe->phfg", query4, key4, preferred_element_type=jnp.float32) * factor
    )
    logits = jnp.where(allowed, logits, jnp.float32(-1e30))
    shifted = jnp.exp(logits - jnp.max(logits, axis=-1, keepdims=True))
    probs = shifted / jnp.sum(shifted, axis=-1, keepdims=True)
    probs_low = probs.astype(jnp.bfloat16)
    mixed = jnp.einsum(
        "phfg,gphe->fphe", probs_low, value4, preferred_element_type=jnp.float32
    ).astype(jnp.bfloat16)
    return (probs, probs_low, mixed)


def attend_backward(probs, probs_low, mixed, grad4, query4, key4, value4, factor):
    value_grad = jnp.einsum(
        "phfg,fphe->gphe", probs_low, grad4, preferred_element_type=jnp.float32
    ).astype(jnp.bfloat16)
    through = jnp.einsum("fphe,gphe->phfg", grad4, value4, preferred_element_type=jnp.float32)
    inner = jnp.einsum("fphe,fphe->phf", grad4, mixed, preferred_element_type=jnp.float32)[
        ..., None
    ]
    score_grad = (probs * (through - inner)).astype(jnp.bfloat16)
    query_grad = (
        jnp.einsum("phfg,gphe->fphe", score_grad, key4, preferred_element_type=jnp.float32) * factor
    ).astype(jnp.bfloat16)
    key_grad = (
        jnp.einsum("phfg,fphe->gphe", score_grad, query4, preferred_element_type=jnp.float32)
        * factor
    ).astype(jnp.bfloat16)
    return (query_grad, key_grad, value_grad)


def local(queries, key_field, value_field, out_grad, out_weight, frame_video):
    width_all = queries.shape[3]
    out_width = out_grad.shape[3]
    head_count = width_all // HEAD
    factor = HEAD ** (-0.5)
    q_space, k_space, v_space = (
        lax.all_to_all(queries, "seq", split_axis=2, concat_axis=1, tiled=True),
        lax.all_to_all(key_field, "seq", split_axis=2, concat_axis=1, tiled=True),
        lax.all_to_all(value_field, "seq", split_axis=2, concat_axis=1, tiled=True),
    )
    frame_count = q_space.shape[1]
    place_count = q_space.shape[2]
    four_shape = (frame_count, place_count, head_count, HEAD)
    query4 = q_space.reshape(four_shape)
    key4 = k_space.reshape(four_shape)
    value4 = v_space.reshape(four_shape)
    videos = frame_video[0]
    allowed = (videos[:, None] == videos[None, :])[None, None]
    probs, probs_low, mixed = attend_forward(query4, key4, value4, allowed, factor)
    mixed_frames = lax.all_to_all(
        mixed.reshape(q_space.shape), "seq", split_axis=1, concat_axis=2, tiled=True
    )
    row_count = mixed_frames.shape[1] * mixed_frames.shape[2]
    mixed_flat = mixed_frames.reshape(row_count, width_all)
    grad_flat = out_grad.reshape(row_count, out_width)
    contract_cols = (((1,), (1,)), ((), ()))
    columns = mixed_flat
    out_flat = jnp.dot(
        columns,
        lax.all_gather(out_weight, "seq", axis=0, tiled=True),
        preferred_element_type=jnp.float32,
    )
    mixed_grad = lax.dot_general(
        grad_flat,
        lax.all_gather(out_weight, "seq", axis=0, tiled=True),
        contract_cols,
        preferred_element_type=jnp.float32,
    )
    mixed_out = out_flat.astype(jnp.bfloat16).reshape(out_grad.shape)
    grad_frames = mixed_grad.astype(jnp.bfloat16).reshape(queries.shape)
    grad_space = lax.all_to_all(grad_frames, "seq", split_axis=2, concat_axis=1, tiled=True)
    grad4 = grad_space.reshape(four_shape)
    query_grad, key_grad, value_grad = attend_backward(
        probs, probs_low, mixed, grad4, query4, key4, value4, factor
    )
    q_back, k_back, v_back = (
        lax.all_to_all(
            query_grad.reshape(q_space.shape), "seq", split_axis=1, concat_axis=2, tiled=True
        ),
        lax.all_to_all(
            key_grad.reshape(q_space.shape), "seq", split_axis=1, concat_axis=2, tiled=True
        ),
        lax.all_to_all(
            value_grad.reshape(q_space.shape), "seq", split_axis=1, concat_axis=2, tiled=True
        ),
    )
    contract_rows = (((0,), (0,)), ((), ()))
    columns = mixed_flat
    group_share = lax.psum_scatter(
        lax.dot_general(columns, grad_flat, contract_rows, preferred_element_type=jnp.float32),
        "seq",
        scatter_dimension=0,
        tiled=True,
    )
    weight_grad = lax.psum(group_share.astype(jnp.bfloat16), "dp").astype(jnp.float32)
    return (mixed_out, q_back, k_back, v_back, weight_grad)


def solution(mesh):
    placed = (
        P("dp", "seq", None, None),
        P("dp", "seq", None, None),
        P("dp", "seq", None, None),
        P("dp", "seq", None, None),
        P("seq", None),
        P("dp", None),
    )
    return jax.shard_map(
        local,
        mesh=mesh,
        in_specs=placed,
        out_specs=(
            P("dp", "seq", None, None),
            P("dp", "seq", None, None),
            P("dp", "seq", None, None),
            P("dp", "seq", None, None),
            P("seq", None),
        ),
        check_vma=False,
    )
```

profile of v0, /device:TPU:0, one launch (start us, length us, event | category | flops | bytes accessed | tf_op | source)
XLA Modules:
  0.0 257.0 jit_solution(6479106536022073896)
XLA Ops:
  7.2 0.7 all-gather.2.cloned.1.call-update
  7.9 1.1 copy.101
  9.1 0.5 broadcast.35
  9.6 1.5 reduce.13
  11.1 0.8 reshape.135
  11.8 7.4 %all-to-all-start = ((bf16[16,2,2304]{2,1,0:T(2,128)(2,1)}), bf16[16,2,2304]{2,1,0:T(2,128)(2,1)S(1)}, u32[]{:S(2)}, u32[]{:S(2)}) async-start(bf16[16,2,2304]{2,1,0:T(2,128)(2,1)} %reshape.135), calls=%async_computation | async-start | bytes 294912 | tf_op jit(solution)/shard_map/all_to_all | solution.py:48
  19.2 1.1 copy.100
  20.4 1.5 reduce.12
  21.9 0.8 reshape.133
  22.6 6.0 %all-to-all-done = bf16[16,2,2304]{2,1,0:T(2,128)(2,1)S(1)} async-done(((bf16[16,2,2304]{2,1,0:T(2,128)(2,1)}), bf16[16,2,2304]{2,1,0:T(2,128)(2,1)S(1)}, u32[]{:S(2)}, u32[]{:S(2)}) %all-to-all-start) | async-done | bytes 147488 | tf_op jit(solution)/shard_map/all_to_all | solution.py:48
  28.7 4.3 %all-to-all-start.1 = ((bf16[16,2,2304]{2,1,0:T(2,128)(2,1)}), bf16[16,2,2304]{2,1,0:T(2,128)(2,1)S(1)}, u32[]{:S(2)}, u32[]{:S(2)}) async-start(bf16[16,2,2304]{2,1,0:T(2,128)(2,1)} %reshape.133), calls=%async_computation.1 | async-start | bytes 294912 | tf_op jit(solution)/shard_map/all_to_all | solution.py:49
  33.0 1.1 copy.99
  34.1 1.5 reduce.11
  35.6 0.8 reshape.131
  36.4 0.8 broadcast_compare_fusion
  37.3 3.9 %all-to-all-done.1 = bf16[16,2,2304]{2,1,0:T(2,128)(2,1)S(1)} async-done(((bf16[16,2,2304]{2,1,0:T(2,128)(2,1)}), bf16[16,2,2304]{2,1,0:T(2,128)(2,1)S(1)}, u32[]{:S(2)}, u32[]{:S(2)}) %all-to-all-start.1) | async-done | bytes 147488 | tf_op jit(solution)/shard_map/all_to_all | solution.py:49
  41.2 3.5 %all-to-all-start.2 = ((bf16[16,2,2304]{2,1,0:T(2,128)(2,1)}), bf16[16,2,2304]{2,1,0:T(2,128)(2,1)S(1)}, u32[]{:S(2)}, u32[]{:S(2)}) async-start(bf16[16,2,2304]{2,1,0:T(2,128)(2,1)} %reshape.131), calls=%async_computation.2 | async-start | bytes 294912 | tf_op jit(solution)/shard_map/all_to_all | solution.py:50
  44.7 0.8 bitcast_reduce_fusion.1
  45.8 0.8 bitcast_reduce_fusion.2
  46.7 8.9 %all-to-all-done.2 = bf16[16,2,2304]{2,1,0:T(2,128)(2,1)S(1)} async-done(((bf16[16,2,2304]{2,1,0:T(2,128)(2,1)}), bf16[16,2,2304]{2,1,0:T(2,128)(2,1)S(1)}, u32[]{:S(2)}, u32[]{:S(2)}) %all-to-all-start.2) | async-done | bytes 147488 | tf_op jit(solution)/shard_map/all_to_all | solution.py:50
  55.9 15.0 %all-gather.2.cloned.1.call-done = bf16[1536,1536]{1,0:T(8,128)(2,1)} async-done(((bf16[96,1536]{1,0:T(8,128)(2,1)}), bf16[1536,1536]{1,0:T(8,128)(2,1)}) %all-gather.2.cloned.1.call-update) | async-done | bytes 4718608 | tf_op jit(solution)/shard_map/all_gather | solution.py:71
  70.9 3.8 %fusion.2 = bf16[1,1,48,1536]{3,2,1,0:T(8,128)(2,1)S(1)} fusion(bf16[1536,1536]{1,0:T(8,128)(2,1)} %all-gather.2.cloned.1.call-done, bf16[1,1,48,1536]{3,2,1,0:T(8,128)(2,1)S(1)} %copy-done), kind=kOutput, calls=%fused_computation.4 | convolution fusion | flops 226566144 | bytes 5013504 | tf_op jit(solution)/shard_map/dot_general | solution.py:74
  75.0 1.5 reduce.10
  76.5 0.8 reshape.137
  77.3 3.5 %all-to-all-start.4 = ((bf16[16,2,2304]{2,1,0:T(2,128)(2,1)}), bf16[16,2,2304]{2,1,0:T(2,128)(2,1)S(1)}, u32[]{:S(2)}, u32[]{:S(2)}) async-start(bf16[16,2,2304]{2,1,0:T(2,128)(2,1)} %reshape.137), calls=%async_computation.4 | async-start | bytes 294912 | tf_op jit(solution)/shard_map/all_to_all | solution.py:82
  81.0 0.8 bitcast_reduce_fusion.3
  82.0 1.3 fusion.27
  83.2 5.7 %all-to-all-done.4 = bf16[16,2,2304]{2,1,0:T(2,128)(2,1)S(1)} async-done(((bf16[16,2,2304]{2,1,0:T(2,128)(2,1)}), bf16[16,2,2304]{2,1,0:T(2,128)(2,1)S(1)}, u32[]{:S(2)}, u32[]{:S(2)}) %all-to-all-start.4) | async-done | bytes 147488 | tf_op jit(solution)/shard_map/all_to_all | solution.py:82
  89.1 0.8 bitcast_reduce_fusion
  90.5 11.6 %all_to_all.81 = bf16[1,16,3,1536]{3,2,0,1:T(4,128)(2,1)S(1)} all-to-all(bf16[1,16,3,1536]{3,2,0,1:T(4,128)(2,1)S(1)} %reshape.123), channel_id=1, replica_groups=mesh['dp'=2,'seq'=16] {'seq'}, dimensions={1} | all-to-all | bytes 294912 | tf_op jit(solution)/shard_map/all_to_all | solution.py:61
  102.3 5.0 %fusion.13 = f32[1536,1536]{1,0:T(8,128)} fusion(bf16[48,1536]{1,0:T(8,128)(2,1)S(1)} %reshape.112, bf16[1,1,48,1536]{3,2,1,0:T(8,128)(2,1)S(1)} %copy-done), kind=kOutput, calls=%fused_computation.23 | convolution fusion | flops 226492416 | bytes 9732096 | tf_op jit(solution)/shard_map/dot_general | solution.py:101
  107.7 0.8 reshape.126
  108.4 3.5 %all-to-all-start.7 = ((bf16[1,16,3,1536]{3,2,0,1:T(4,128)(2,1)}), bf16[1,16,3,1536]{3,2,0,1:T(4,128)(2,1)S(1)}, u32[]{:S(2)}, u32[]{:S(2)}) async-start(bf16[1,16,3,1536]{3,2,0,1:T(4,128)(2,1)} %reshape.126), calls=%async_computation.7 | async-start | bytes 393216 | tf_op jit(solution)/shard_map/all_to_all | solution.py:94
  112.5 0.7 reshape.124
  113.2 7.7 %all-to-all-done.7 = bf16[1,16,3,1536]{3,2,0,1:T(4,128)(2,1)S(1)} async-done(((bf16[1,16,3,1536]{3,2,0,1:T(4,128)(2,1)}), bf16[1,16,3,1536]{3,2,0,1:T(4,128)(2,1)S(1)}, u32[]{:S(2)}, u32[]{:S(2)}) %all-to-all-start.7) | async-done | bytes 147488 | tf_op jit(solution)/shard_map/all_to_all | solution.py:94
  120.9 3.5 %all-to-all-start.5 = ((bf16[1,16,3,1536]{3,2,0,1:T(4,128)(2,1)}), bf16[1,16,3,1536]{3,2,0,1:T(4,128)(2,1)S(1)}, u32[]{:S(2)}, u32[]{:S(2)}) async-start(bf16[1,16,3,1536]{3,2,0,1:T(4,128)(2,1)} %reshape.124), calls=%async_computation.5 | async-start | bytes 393216 | tf_op jit(solution)/shard_map/all_to_all | solution.py:88
  124.7 0.8 reshape.125
  125.5 7.9 %all-to-all-done.5 = bf16[1,16,3,1536]{3,2,0,1:T(4,128)(2,1)S(1)} async-done(((bf16[1,16,3,1536]{3,2,0,1:T(4,128)(2,1)}), bf16[1,16,3,1536]{3,2,0,1:T(4,128)(2,1)S(1)}, u32[]{:S(2)}, u32[]{:S(2)}) %all-to-all-start.5) | async-done | bytes 147488 | tf_op jit(solution)/shard_map/all_to_all | solution.py:88
  133.4 3.5 %all-to-all-start.6 = ((bf16[1,16,3,1536]{3,2,0,1:T(4,128)(2,1)}), bf16[1,16,3,1536]{3,2,0,1:T(4,128)(2,1)S(1)}, u32[]{:S(2)}, u32[]{:S(2)}) async-start(bf16[1,16,3,1536]{3,2,0,1:T(4,128)(2,1)} %reshape.125), calls=%async_computation.6 | async-start | bytes 393216 | tf_op jit(solution)/shard_map/all_to_all | solution.py:91
  137.0 0.8 all_to_all.32
  137.8 0.8 all_to_all.28
  138.6 10.5 %all-to-all-done.6 = bf16[1,16,3,1536]{3,2,0,1:T(4,128)(2,1)S(1)} async-done(((bf16[1,16,3,1536]{3,2,0,1:T(4,128)(2,1)}), bf16[1,16,3,1536]{3,2,0,1:T(4,128)(2,1)S(1)}, u32[]{:S(2)}, u32[]{:S(2)}) %all-to-all-start.6) | async-done | bytes 147488 | tf_op jit(solution)/shard_map/all_to_all | solution.py:91
  149.0 0.8 all_to_all.30
  149.8 72.5 %reduce-scatter.2.cloned.1.call-done = f32[96,1536]{1,0:T(8,128)} async-done(((f32[1536,1536]{1,0:T(8,128)}), f32[96,1536]{1,0:T(8,128)}) %reduce-scatter.2.cloned.1.call-update) | async-done | bytes 589840 | tf_op jit(solution)/shard_map/reduce_scatter | solution.py:100
  222.3 1.8 convert_element_type.54
  224.1 3.9 %fusion.1 = bf16[1,1,48,1536]{3,2,1,0:T(8,128)(2,1)} fusion(bf16[48,1536]{1,0:T(8,128)(2,1)S(1)} %reshape.112, bf16[1536,1536]{1,0:T(8,128)(2,1)} %all-gather.2.cloned.1.call-done), kind=kOutput, calls=%fused_computation.3 | convolution fusion | flops 226566144 | bytes 5013504 | tf_op jit(solution)/shard_map/dot_general | solution.py:69
  228.0 20.6 %all-reduce.2.cloned.1.call-done = bf16[96,1536]{1,0:T(8,128)(2,1)} async-done(((bf16[96,1536]{1,0:T(8,128)(2,1)}), bf16[96,1536]{1,0:T(8,128)(2,1)}) %all-reduce.2.cloned.1.call-update) | async-done | bytes 294928 | tf_op jit(solution)/shard_map/psum | solution.py:106
  248.7 1.8 convert_element_type.55
  (29 shorter events, 3.4 us)
Async XLA Ops:
  7.2 63.8 %copy-start = (bf16[1,1,48,1536]{3,2,1,0:T(8,128)(2,1)S(1)}, bf16[1,1,48,1536]{3,2,1,0:T(8,128)(2,1)}, u32[]{:S(2)}) copy-start(bf16[1,1,48,1536]{3,2,1,0:T(8,128)(2,1)} %param.9) | copy-start | bytes 442372
  7.2 63.8 %all-gather.2.cloned.1.call-start = ((), (), s32[]{:S(2)}) async-start(), calls=%async_computation.9 | async-start | bytes 5013504 | tf_op jit(solution)/shard_map/all_gather | solution.py:71
  11.8 16.8 %all-to-all-start = ((bf16[16,2,2304]{2,1,0:T(2,128)(2,1)}), bf16[16,2,2304]{2,1,0:T(2,128)(2,1)S(1)}, u32[]{:S(2)}, u32[]{:S(2)}) async-start(bf16[16,2,2304]{2,1,0:T(2,128)(2,1)} %reshape.135), calls=%async_computation | async-start | bytes 294912 | tf_op jit(solution)/shard_map/all_to_all | solution.py:48
  28.7 12.5 %all-to-all-start.1 = ((bf16[16,2,2304]{2,1,0:T(2,128)(2,1)}), bf16[16,2,2304]{2,1,0:T(2,128)(2,1)S(1)}, u32[]{:S(2)}, u32[]{:S(2)}) async-start(bf16[16,2,2304]{2,1,0:T(2,128)(2,1)} %reshape.133), calls=%async_computation.1 | async-start | bytes 294912 | tf_op jit(solution)/shard_map/all_to_all | solution.py:49
  41.2 14.4 %all-to-all-start.2 = ((bf16[16,2,2304]{2,1,0:T(2,128)(2,1)}), bf16[16,2,2304]{2,1,0:T(2,128)(2,1)S(1)}, u32[]{:S(2)}, u32[]{:S(2)}) async-start(bf16[16,2,2304]{2,1,0:T(2,128)(2,1)} %reshape.131), calls=%async_computation.2 | async-start | bytes 294912 | tf_op jit(solution)/shard_map/all_to_all | solution.py:50
  77.3 11.7 %all-to-all-start.4 = ((bf16[16,2,2304]{2,1,0:T(2,128)(2,1)}), bf16[16,2,2304]{2,1,0:T(2,128)(2,1)S(1)}, u32[]{:S(2)}, u32[]{:S(2)}) async-start(bf16[16,2,2304]{2,1,0:T(2,128)(2,1)} %reshape.137), calls=%async_computation.4 | async-start | bytes 294912 | tf_op jit(solution)/shard_map/all_to_all | solution.py:82
  80.8 141.5 %reduce-scatter.2.cloned.1.call-start = ((), (), s32[]{:S(2)}) async-start(), calls=%async_computation.10 | async-start | bytes 10027008 | tf_op jit(solution)/shard_map/reduce_scatter | solution.py:100
  108.4 12.5 %all-to-all-start.7 = ((bf16[1,16,3,1536]{3,2,0,1:T(4,128)(2,1)}), bf16[1,16,3,1536]{3,2,0,1:T(4,128)(2,1)S(1)}, u32[]{:S(2)}, u32[]{:S(2)}) async-start(bf16[1,16,3,1536]{3,2,0,1:T(4,128)(2,1)} %reshape.126), calls=%async_computation.7 | async-start | bytes 393216 | tf_op jit(solution)/shard_map/all_to_all | solution.py:94
  120.9 12.5 %all-to-all-start.5 = ((bf16[1,16,3,1536]{3,2,0,1:T(4,128)(2,1)}), bf16[1,16,3,1536]{3,2,0,1:T(4,128)(2,1)S(1)}, u32[]{:S(2)}, u32[]{:S(2)}) async-start(bf16[1,16,3,1536]{3,2,0,1:T(4,128)(2,1)} %reshape.124), calls=%async_computation.5 | async-start | bytes 393216 | tf_op jit(solution)/shard_map/all_to_all | solution.py:88
  133.4 15.6 %all-to-all-start.6 = ((bf16[1,16,3,1536]{3,2,0,1:T(4,128)(2,1)}), bf16[1,16,3,1536]{3,2,0,1:T(4,128)(2,1)S(1)}, u32[]{:S(2)}, u32[]{:S(2)}) async-start(bf16[1,16,3,1536]{3,2,0,1:T(4,128)(2,1)} %reshape.125), calls=%async_computation.6 | async-start | bytes 393216 | tf_op jit(solution)/shard_map/all_to_all | solution.py:91
  136.9 111.7 %all-reduce.2.cloned.1.call-start = ((), (), s32[]{:S(2)}) async-start(), calls=%async_computation.11 | async-start | bytes 589824 | tf_op jit(solution)/shard_map/psum | solution.py:106
Sparse Core Ops, SparseCore 0:
  10.3 60.5 all-gather.1
  107.5 114.7 reduce-scatter.1
  225.2 23.3 all-reduce.1
where the time goes:
time: 258 us; the launch traced here: 257 us
  waiting for transfers between devices  159 us (62%)
  starting transfers between devices  29.6 us (11%)
  local copies, waits for them, and re-layouts  16.3 us (6%)
  matrix products  14.3 us (6%)
  between operations  14 us (5%)
  other arithmetic  11.7 us (5%)
  blocking collectives  11.6 us (4%)
    reduce_scatter x1, waiting for transfers between devices, local(): lax.psum_scatter(lax.dot_general(columns, grad_flat, contract_rows, prefe...  72.5 us
    psum x1, waiting for transfers between devices, local(): lax.psum(group_share.astype(jnp.bfloat16), 'dp').astype(jnp.float32)  20.6 us
    all_gather x1, waiting for transfers between devices, local(): lax.all_gather(out_weight, 'seq', axis=0, tiled=True)  15 us
    all_to_all x1, blocking collectives, local(): lax.all_to_all(mixed.reshape(q_space.shape), 'seq', split_axis=1, concat_...  11.6 us
    all_to_all x1, waiting for transfers between devices, local(): lax.all_to_all(key_grad.reshape(q_space.shape), 'seq', split_axis=1, conc...  10.5 us
    all_to_all x1, waiting for transfers between devices, local(): lax.all_to_all(value_field, 'seq', split_axis=2, concat_axis=1, tiled=True)  8.87 us
    all_to_all x1, waiting for transfers between devices, local(): lax.all_to_all(query_grad.reshape(q_space.shape), 'seq', split_axis=1, co...  7.94 us
    all_to_all x1, waiting for transfers between devices, local(): lax.all_to_all(value_grad.reshape(q_space.shape), 'seq', split_axis=1, co...  7.69 us
  transfers between devices with their start and end apart: 10, of which 10 were waited for; matrix products, arithmetic and copies ran while one was open for 9% of the time, Pallas kernels for 0%

commit v1 on v0

v1 whole, which is shorter than its diff:
```python
import jax
import jax.numpy as jnp
from jax import lax
from jax.sharding import PartitionSpec as P

HEAD = 128
LOW = jnp.bfloat16


def dot(a, b, dims):
    return lax.dot_general(a, b, dims, preferred_element_type=jnp.float32)


def exchange(blocks):
    return lax.all_to_all(blocks, "seq", split_axis=0, concat_axis=0, tiled=True)


def local(queries, key_field, value_field, out_grad, out_weight, frame_video):
    n = lax.axis_size("seq")
    _, own, span, width = queries.shape
    frames = own * n
    per = span // n
    heads = width // HEAD
    rows = own * per * heads
    part = out_weight.shape[0]
    factor = HEAD ** (-0.5)

    def to_blocks(x):
        return x[0].reshape(own, n, per * heads, HEAD).swapaxes(0, 1).reshape(n, rows, HEAD)

    def to_places(x):
        return (
            x.reshape(frames, per, heads, HEAD)
            .swapaxes(0, 1)
            .reshape(per, frames * heads, HEAD)
        )

    def to_frames(x):
        return x.reshape(per, frames, heads, HEAD).swapaxes(0, 1).reshape(n, rows, HEAD)

    def from_blocks(x):
        return x.reshape(n, own, per, width).swapaxes(0, 1).reshape(1, own, span, width)

    grad_all = lax.all_gather(out_grad[0], "seq", axis=0, tiled=True)
    grad_all = grad_all.reshape(frames * span, out_grad.shape[3])

    spread = exchange(
        jnp.concatenate([to_blocks(x) for x in (queries, key_field, value_field)], axis=1)
    )
    query, key, value = (
        to_places(spread[:, i * rows : (i + 1) * rows]) for i in range(3)
    )

    videos = jnp.repeat(frame_video[0], heads)
    head_of = jnp.tile(jnp.arange(heads, dtype=jnp.int32), frames)
    allowed = (videos[:, None] == videos[None, :]) & (head_of[:, None] == head_of[None, :])
    inside = (((2,), (2,)), ((0,), (0,)))
    onward = (((2,), (1,)), ((0,), (0,)))
    across = (((1,), (1,)), ((0,), (0,)))
    logits = jnp.where(allowed[None], dot(query, key, inside) * factor, jnp.float32(-1e30))
    shifted = jnp.exp(logits - jnp.max(logits, axis=-1, keepdims=True))
    probs = shifted / jnp.sum(shifted, axis=-1, keepdims=True)
    probs_low = probs.astype(LOW)
    mixed = dot(probs_low, value, onward).astype(LOW)

    mixed_frames = to_frames(mixed)
    by_feature = mixed_frames.reshape(frames * per, n, part).swapaxes(0, 1)
    by_feature = jnp.pad(by_feature, ((0, 0), (0, 0), (0, HEAD - part)))
    back = exchange(jnp.concatenate([mixed_frames, by_feature], axis=1))
    mixed_rows = from_blocks(back[:, :rows]).reshape(own * span, width)
    mixed_part = (
        back[:, rows:, :part]
        .reshape(n, frames, per, part)
        .swapaxes(0, 1)
        .reshape(frames * span, part)
    )

    out_weight_later, grad_all = lax.optimization_barrier((out_weight, grad_all))
    weight_all = lax.all_gather(out_weight_later, "seq", axis=0, tiled=True)

    mixed_grad = dot(grad_all, out_weight, (((1,), (1,)), ((), ()))).astype(LOW)
    mixed_grad = (
        mixed_grad.reshape(frames, n, per, part).swapaxes(0, 1).reshape(n, frames * per, part)
    )
    grad = to_places(exchange(mixed_grad).swapaxes(0, 1).reshape(frames, per, width))

    value_grad = dot(probs_low, grad, across).astype(LOW)
    through = dot(grad, value, inside)
    inner = jnp.sum(
        grad.astype(jnp.float32) * mixed.astype(jnp.float32), axis=-1, keepdims=True
    )
    score_grad = (probs * (through - inner)).astype(LOW)
    query_grad = (dot(score_grad, key, onward) * factor).astype(LOW)
    key_grad = (dot(score_grad, query, across) * factor).astype(LOW)
    home = exchange(
        jnp.concatenate([to_frames(x) for x in (query_grad, key_grad, value_grad)], axis=1)
    )
    q_back, k_back, v_back = (
        from_blocks(home[:, i * rows : (i + 1) * rows]) for i in range(3)
    )

    share = dot(mixed_part, grad_all, (((0,), (0,)), ((), ()))).astype(LOW)
    if lax.axis_size("dp") == 2:
        other = lax.ppermute(share, "dp", [(0, 1), (1, 0)])
        weight_grad = share.astype(jnp.float32) + other.astype(jnp.float32)
    else:
        weight_grad = lax.psum(share, "dp").astype(jnp.float32)

    mixed_out = dot(mixed_rows, weight_all, (((1,), (0,)), ((), ()))).astype(LOW)
    return (mixed_out.reshape(out_grad.shape), q_back, k_back, v_back, weight_grad)


def solution(mesh):
    placed = (
        P("dp", "seq", None, None),
        P("dp", "seq", None, None),
        P("dp", "seq", None, None),
        P("dp", "seq", None, None),
        P("seq", None),
        P("dp", None),
    )
    return jax.shard_map(
        local,
        mesh=mesh,
        in_specs=placed,
        out_specs=(
            P("dp", "seq", None, None),
            P("dp", "seq", None, None),
            P("dp", "seq", None, None),
            P("dp", "seq", None, None),
            P("seq", None),
        ),
        check_vma=False,
    )
```

time: 258 us -> 157 us (0.61)
  waiting for transfers between devices: 159 us -> 95.2 us
  blocking collectives: 11.6 us -> 0 us
  other arithmetic: 11.7 us -> 1.98 us
  starting transfers between devices: 29.6 us -> 21.3 us
  local copies, waits for them, and re-layouts: 16.3 us -> 11.6 us
  matrix products: 14.3 us -> 11.6 us
    reduce_scatter x1 -> x0, waiting for transfers between devices: 72.5 us -> none  [local(): lax.psum_scatter(lax.dot_general(columns, grad_flat, contract_rows, prefe...]
    all_gather x1 -> x2, waiting for transfers between devices: 15 us -> 47.3 us  [the longest x1 47.3 us: local(): grad_all = lax.all_gather(out_grad[0], 'seq', axis=0, tiled=True)]
    psum x1 -> x0, waiting for transfers between devices: 20.6 us -> none  [local(): lax.psum(group_share.astype(jnp.bfloat16), 'dp').astype(jnp.float32)]
    all_to_all x1 -> x0, blocking collectives: 11.6 us -> none  [local(): lax.all_to_all(mixed.reshape(q_space.shape), 'seq', split_axis=1, concat_...]
    all_to_all x7 -> x4, starting transfers between devices: 29.3 us -> 19.7 us  [exchange(): lax.all_to_all(blocks, 'seq', split_axis=0, concat_axis=0, tiled=True)]
    unnamed x14 -> x21, local copies, waits for them, and re-layouts: 7.43 us -> 0.1 us
    another operation x0 -> x10, local copies, waits for them, and re-layouts: none -> 6.58 us  [the longest x3 3.49 us: to_blocks(): x[0].reshape(own, n, per * heads, HEAD).swapaxes(0, 1)]
    unnamed x5 -> x0, other arithmetic: 6.01 us -> none
  transfers between devices with their start and end apart: 10 -> 7, of which waited for: 10 -> 5; matrix products, arithmetic and copies ran while one was open for 9% -> 14% of each run, Pallas kernels for 0% -> 0%
where the time goes in v1:
time: 157 us; the launch traced here: 156 us
  waiting for transfers between devices  95.2 us (61%)
  starting transfers between devices  21.3 us (14%)
  between operations  14.5 us (9%)
  local copies, waits for them, and re-layouts  11.6 us (7%)
  matrix products  11.6 us (7%)
  other arithmetic  1.98 us (1%)
    all_gather x1, waiting for transfers between devices, local(): grad_all = lax.all_gather(out_grad[0], 'seq', axis=0, tiled=True)  47.3 us
    all_to_all x4, waiting for transfers between devices, exchange(): lax.all_to_all(blocks, 'seq', split_axis=0, concat_axis=0, tiled=True)  47.3 us
    all_to_all x4, starting transfers between devices, exchange(): lax.all_to_all(blocks, 'seq', split_axis=0, concat_axis=0, tiled=True)  19.7 us
    dot_general x8, matrix products, dot(): return lax.dot_general(a, b, dims, preferred_element_type=jnp.float32)  10.5 us
    another operation x3, local copies, waits for them, and re-layouts, to_blocks(): x[0].reshape(own, n, per * heads, HEAD).swapaxes(0, 1)  3.49 us
  transfers between devices with their start and end apart: 7, of which 5 were waited for; matrix products, arithmetic and copies ran while one was open for 14% of the time, Pallas kernels for 0%

profile of v1, /device:TPU:0, one launch (start us, length us, event | category | flops | bytes accessed | tf_op | source)
XLA Modules:
  0.0 156.3 jit_solution(4705356074791134661)
XLA Ops:
  7.2 0.7 all-gather.6.cloned.1.call-update
  8.0 47.3 %all-gather.6.cloned.1.call-done = bf16[16,1,48,1536]{3,2,1,0:T(8,128)(2,1)} async-done(((bf16[1,1,48,1536]{3,2,1,0:T(8,128)(2,1)}), bf16[16,1,48,1536]{3,2,1,0:T(8,128)(2,1)}) %all-gather.6.cloned.1.call-update) | async-done | bytes 2359312 | tf_op jit(solution)/shard_map/all_gather | solution.py:44
  55.3 1.3 reshape_transpose_reshape_squeeze.10
  56.5 1.1 reshape_transpose_reshape_squeeze.11
  57.7 1.1 reshape_transpose_reshape_squeeze.9
  58.8 0.8 pad_maximum_fusion
  59.6 3.6 %all-to-all-start = ((bf16[16,108,128]{2,1,0:T(8,128)(2,1)}), bf16[16,108,128]{2,1,0:T(8,128)(2,1)S(1)}, u32[]{:S(2)}, u32[]{:S(2)}) async-start(bf16[16,108,128]{2,1,0:T(8,128)(2,1)} %pad_maximum_fusion), calls=%async_computation | async-start | bytes 917504 | tf_op jit(solution)/shard_map/all_to_all | solution.py:15
  63.2 0.1 broadcast_in_dim.19
  63.3 0.1 eq.38
  63.4 0.1 eq.42
  63.5 0.1 compare_and_fusion
  63.6 0.8 convolution_convert_fusion.3
  64.5 0.2 copy.69
  64.6 0.1 reshape.153
  64.8 0.7 copy.71
  65.6 17.7 %all-to-all-done = bf16[16,108,128]{2,1,0:T(8,128)(2,1)S(1)} async-done(((bf16[16,108,128]{2,1,0:T(8,128)(2,1)}), bf16[16,108,128]{2,1,0:T(8,128)(2,1)S(1)}, u32[]{:S(2)}, u32[]{:S(2)}) %all-to-all-start) | async-done | bytes 442400 | tf_op jit(solution)/shard_map/all_to_all | solution.py:15
  83.2 6.0 %all-to-all-start.2 = ((bf16[16,48,96]{2,1,0:T(8,128)(2,1)}), bf16[16,48,96]{2,1,0:T(8,128)(2,1)S(1)}, u32[]{:S(2)}, u32[]{:S(2)}) async-start(bf16[16,48,96]{2,1,0:T(8,128)(2,1)} %copy.71), calls=%async_computation.2 | async-start | bytes 393216 | tf_op jit(solution)/shard_map/all_to_all | solution.py:15
  89.2 0.1 fusion.18
  89.7 1.2 fusion.19
  90.9 9.9 %all-to-all-done.2 = bf16[16,48,96]{2,1,0:T(8,128)(2,1)S(1)} async-done(((bf16[16,48,96]{2,1,0:T(8,128)(2,1)}), bf16[16,48,96]{2,1,0:T(8,128)(2,1)S(1)}, u32[]{:S(2)}, u32[]{:S(2)}) %all-to-all-start.2) | async-done | bytes 147488 | tf_op jit(solution)/shard_map/all_to_all | solution.py:15
  100.9 0.1 copy.72
  100.9 0.2 reshape_reshape.7
  101.2 0.7 multiply_reduce_fusion
  102.0 0.2 reshape_reshape.6
  102.2 0.1 fusion.10
  102.3 0.8 copy.68
  103.1 5.2 %all-to-all-start.1 = ((bf16[16,84,128]{2,1,0:T(8,128)(2,1)}), bf16[16,84,128]{2,1,0:T(8,128)(2,1)S(1)}, u32[]{:S(2)}, u32[]{:S(2)}) async-start(bf16[16,84,128]{2,1,0:T(8,128)(2,1)} %copy.68), calls=%async_computation.1 | async-start | bytes 720896 | tf_op jit(solution)/shard_map/all_to_all | solution.py:15
  108.4 1.5 fusion.6
  109.9 0.3 fusion.7
  110.3 0.2 fusion.8
  110.6 1.5 convolution_convert_fusion.2
  112.3 0.9 copy.79
  113.2 10.7 %all-to-all-done.1 = bf16[16,84,128]{2,1,0:T(8,128)(2,1)S(1)} async-done(((bf16[16,84,128]{2,1,0:T(8,128)(2,1)}), bf16[16,84,128]{2,1,0:T(8,128)(2,1)S(1)}, u32[]{:S(2)}, u32[]{:S(2)}) %all-to-all-start.1) | async-done | bytes 344096 | tf_op jit(solution)/shard_map/all_to_all | solution.py:15
  123.9 4.9 %all-to-all-start.3 = ((bf16[16,108,128]{2,1,0:T(8,128)(2,1)}), bf16[16,108,128]{2,1,0:T(8,128)(2,1)S(1)}, u32[]{:S(2)}, u32[]{:S(2)}) async-start(bf16[16,108,128]{2,1,0:T(8,128)(2,1)} %copy.79), calls=%async_computation.3 | async-start | bytes 917504 | tf_op jit(solution)/shard_map/all_to_all | solution.py:15
  128.8 0.1 slice.39
  128.9 0.1 copy.85
  128.9 0.1 copy.81
  129.1 0.8 reshape.163
  129.9 1.5 convolution_convert_fusion
  131.4 1.5 collective-permute-start
  132.9 0.2 reshape_reshape_transpose_reshape.3
  133.1 8.9 %all-to-all-done.3 = bf16[16,108,128]{2,1,0:T(8,128)(2,1)S(1)} async-done(((bf16[16,108,128]{2,1,0:T(8,128)(2,1)}), bf16[16,108,128]{2,1,0:T(8,128)(2,1)S(1)}, u32[]{:S(2)}, u32[]{:S(2)}) %all-to-all-start.3) | async-done | bytes 442400 | tf_op jit(solution)/shard_map/all_to_all | solution.py:15
  142.1 0.1 fusion.17
  142.1 0.9 reshape_transpose_reshape.10
  143.0 0.9 reshape_transpose_reshape.11
  143.8 0.9 reshape_transpose_reshape.9
  144.7 0.9 convert_add_fusion
  145.6 3.9 %fusion.1 = bf16[1,1,48,1536]{3,2,1,0:T(8,128)(2,1)} fusion(bf16[48,1536]{1,0:T(8,128)(2,1)S(1)} %reshape_reshape_transpose_reshape.3, bf16[1536,1536]{1,0:T(8,128)(2,1)} %all-gather.4.cloned.1.call-done), kind=kOutput, calls=%fused_computation.3 | convolution fusion | flops 226566144 | bytes 5013504 | tf_op jit(solution)/shard_map/dot_general | solution.py:11
  (49 shorter events, 0.9 us)
Async XLA Ops:
  7.2 56.4 %copy-start.1 = (bf16[96,1536]{1,0:T(8,128)(2,1)S(1)}, bf16[96,1536]{1,0:T(8,128)(2,1)}, u32[]{:S(2)}) copy-start(bf16[96,1536]{1,0:T(8,128)(2,1)} %param.10) | copy-start | bytes 884740
  7.2 56.0 %copy-start.8 = (s32[1,16]{1,0:T(1,128)S(1)}, s32[1,16]{1,0:T(1,128)}, u32[]{:S(2)}) copy-start(s32[1,16]{1,0:T(1,128)} %param.11) | copy-start | bytes 196
  7.2 48.1 %all-gather.6.cloned.1.call-start = ((), (), s32[]{:S(2)}) async-start(), calls=%async_computation.5 | async-start | bytes 2506752 | tf_op jit(solution)/shard_map/all_gather | solution.py:44
  7.9 137.7 %all-gather.4.cloned.1.call-start = ((), (), s32[]{:S(2)}) async-start(), calls=%async_computation.4 | async-start | bytes 5013504 | tf_op jit(solution)/shard_map/all_gather | solution.py:79
  55.3 8.4 %copy-start = (bf16[16,1,48,1536]{3,2,1,0:T(8,128)(2,1)S(1)}, bf16[16,1,48,1536]{3,2,1,0:T(8,128)(2,1)}, u32[]{:S(2)}) copy-start(bf16[16,1,48,1536]{3,2,1,0:T(8,128)(2,1)} %all-gather.6.cloned.1.call-done) | copy-start | bytes 7077892
  59.6 23.6 %all-to-all-start = ((bf16[16,108,128]{2,1,0:T(8,128)(2,1)}), bf16[16,108,128]{2,1,0:T(8,128)(2,1)S(1)}, u32[]{:S(2)}, u32[]{:S(2)}) async-start(bf16[16,108,128]{2,1,0:T(8,128)(2,1)} %pad_maximum_fusion), calls=%async_computation | async-start | bytes 917504 | tf_op jit(solution)/shard_map/all_to_all | solution.py:15
  83.2 17.6 %all-to-all-start.2 = ((bf16[16,48,96]{2,1,0:T(8,128)(2,1)}), bf16[16,48,96]{2,1,0:T(8,128)(2,1)S(1)}, u32[]{:S(2)}, u32[]{:S(2)}) async-start(bf16[16,48,96]{2,1,0:T(8,128)(2,1)} %copy.71), calls=%async_computation.2 | async-start | bytes 393216 | tf_op jit(solution)/shard_map/all_to_all | solution.py:15
  89.4 11.7 %copy-start.2 = (bf16[3,192,128]{2,1,0:T(8,128)(2,1)}, bf16[3,192,128]{2,1,0:T(8,128)(2,1)S(1)}, u32[]{:S(2)}) copy-start(bf16[3,192,128]{2,1,0:T(8,128)(2,1)S(1)} %reshape.144) | copy-start | bytes 442372
  89.6 12.7 %copy-start.4 = (bf16[3,192,128]{2,1,0:T(8,128)(2,1)}, bf16[3,192,128]{2,1,0:T(8,128)(2,1)S(1)}, u32[]{:S(2)}) copy-start(bf16[3,192,128]{2,1,0:T(8,128)(2,1)S(1)} %reshape.146) | copy-start | bytes 442372
  89.7 12.2 %copy-start.7 = (bf16[3,192,128]{2,1,0:T(8,128)(2,1)}, bf16[3,192,128]{2,1,0:T(8,128)(2,1)S(1)}, u32[]{:S(2)}) copy-start(bf16[3,192,128]{2,1,0:T(8,128)(2,1)S(1)} %reshape.148) | copy-start | bytes 442372
  90.9 17.5 %copy-start.9 = (f32[3,192]{1,0:T(4,128)}, f32[3,192]{1,0:T(4,128)S(1)}, u32[]{:S(2)}) copy-start(f32[3,192]{1,0:T(4,128)S(1)} %get-tuple-element.15) | copy-start | bytes 6916
  101.2 0.8 copy-start.6
  103.1 6.7 %copy-start.5 = (bf16[3,192,128]{2,1,0:T(8,128)(2,1)S(1)}, bf16[3,192,128]{2,1,0:T(8,128)(2,1)}, u32[]{:S(2)}) copy-start(bf16[3,192,128]{2,1,0:T(8,128)(2,1)} %copy-done.4) | copy-start | bytes 442372
  103.1 7.2 %copy-start.3 = (bf16[3,192,128]{2,1,0:T(8,128)(2,1)S(1)}, bf16[3,192,128]{2,1,0:T(8,128)(2,1)}, u32[]{:S(2)}) copy-start(bf16[3,192,128]{2,1,0:T(8,128)(2,1)} %copy-done.2) | copy-start | bytes 442372
  103.1 20.7 %all-to-all-start.1 = ((bf16[16,84,128]{2,1,0:T(8,128)(2,1)}), bf16[16,84,128]{2,1,0:T(8,128)(2,1)S(1)}, u32[]{:S(2)}, u32[]{:S(2)}) async-start(bf16[16,84,128]{2,1,0:T(8,128)(2,1)} %copy.68), calls=%async_computation.1 | async-start | bytes 720896 | tf_op jit(solution)/shard_map/all_to_all | solution.py:15
  123.9 18.2 %all-to-all-start.3 = ((bf16[16,108,128]{2,1,0:T(8,128)(2,1)}), bf16[16,108,128]{2,1,0:T(8,128)(2,1)S(1)}, u32[]{:S(2)}, u32[]{:S(2)}) async-start(bf16[16,108,128]{2,1,0:T(8,128)(2,1)} %copy.79), calls=%async_computation.3 | async-start | bytes 917504 | tf_op jit(solution)/shard_map/all_to_all | solution.py:15
  131.4 13.3 %collective-permute-start = (bf16[96,1536]{1,0:T(8,128)(2,1)S(1)}, bf16[96,1536]{1,0:T(8,128)(2,1)S(1)}, u32[]{:S(2)}, u32[]{:S(2)}) collective-permute-start(bf16[96,1536]{1,0:T(8,128)(2,1)S(1)} %convolution_convert_fusion), channel_id=1, source_target_pairs={{0,16},{16,0},{1,17},{17,1},{2,18},{18,2},{3,19},{19,3},{4,20},{20... | collective-permute-start | bytes 884744 | tf_op jit(solution)/shard_map/ppermute | solution.py:104
Sparse Core Ops, SparseCore 0:
  10.3 44.9 all-gather.5
  57.5 68.2 all-gather.3

commit v2 on v1

--- a/solution.py
+++ b/solution.py
@@ -63,20 +63,17 @@
     probs_low = probs.astype(LOW)
     mixed = dot(probs_low, value, onward).astype(LOW)
 
-    mixed_frames = to_frames(mixed)
-    by_feature = mixed_frames.reshape(frames * per, n, part).swapaxes(0, 1)
-    by_feature = jnp.pad(by_feature, ((0, 0), (0, 0), (0, HEAD - part)))
-    back = exchange(jnp.concatenate([mixed_frames, by_feature], axis=1))
-    mixed_rows = from_blocks(back[:, :rows]).reshape(own * span, width)
+    by_feature = to_frames(mixed).reshape(frames * per, n, part).swapaxes(0, 1)
     mixed_part = (
-        back[:, rows:, :part]
+        exchange(by_feature)
         .reshape(n, frames, per, part)
         .swapaxes(0, 1)
         .reshape(frames * span, part)
     )
 
-    out_weight_later, grad_all = lax.optimization_barrier((out_weight, grad_all))
-    weight_all = lax.all_gather(out_weight_later, "seq", axis=0, tiled=True)
+    out_terms = dot(mixed_part, out_weight, (((1,), (0,)), ((), ()))).astype(LOW)
+    mixed_out = lax.psum_scatter(out_terms, "seq", scatter_dimension=0, tiled=True)
+    _, grad_all = lax.optimization_barrier((out_terms, grad_all))
 
     mixed_grad = dot(grad_all, out_weight, (((1,), (1,)), ((), ()))).astype(LOW)
     mixed_grad = (
@@ -106,7 +103,6 @@
     else:
         weight_grad = lax.psum(share, "dp").astype(jnp.float32)
 
-    mixed_out = dot(mixed_rows, weight_all, (((1,), (0,)), ((), ()))).astype(LOW)
     return (mixed_out.reshape(out_grad.shape), q_back, k_back, v_back, weight_grad)
 
 

time: 157 us -> 135 us (0.86)
  waiting for transfers between devices: 95.2 us -> 59.2 us
  blocking collectives: 0 us -> 29.3 us
  starting transfers between devices: 21.3 us -> 12.6 us
  matrix products: 11.6 us -> 7.52 us
  local copies, waits for them, and re-layouts: 11.6 us -> 8.98 us
    all_gather x1, waiting for transfers between devices: 47.3 us -> 2.15 us  [local(): grad_all = lax.all_gather(out_grad[0], 'seq', axis=0, tiled=True)]
    all_to_all x0 -> x2, blocking collectives: none -> 29.3 us  [exchange(): lax.all_to_all(blocks, 'seq', split_axis=0, concat_axis=0, tiled=True)]
    reduce_scatter x0 -> x1, waiting for transfers between devices: none -> 29.1 us  [local(): lax.psum_scatter(out_terms, 'seq', scatter_dimension=0, tiled=True)]
    all_to_all x4 -> x2, waiting for transfers between devices: 47.3 us -> 19.5 us  [exchange(): lax.all_to_all(blocks, 'seq', split_axis=0, concat_axis=0, tiled=True)]
    all_to_all x4 -> x2, starting transfers between devices: 19.7 us -> 10.9 us  [exchange(): lax.all_to_all(blocks, 'seq', split_axis=0, concat_axis=0, tiled=True)]
    ppermute x1, waiting for transfers between devices: 0.01 us -> 7.72 us  [local(): other = lax.ppermute(share, 'dp', [(0, 1), (1, 0)])]
    dot_general x8, matrix products: 10.5 us -> 7.12 us  [dot(): return lax.dot_general(a, b, dims, preferred_element_type=jnp.float32)]
  transfers between devices with their start and end apart: 7 -> 5, of which waited for: 5 -> 5; matrix products, arithmetic and copies ran while one was open for 14% -> 14% of each run, Pallas kernels for 0% -> 0%
where the time goes in v2:
time: 135 us; the launch traced here: 134 us
  waiting for transfers between devices  59.2 us (44%)
  blocking collectives  29.3 us (22%)
  between operations  14.4 us (11%)
  starting transfers between devices  12.6 us (9%)
  local copies, waits for them, and re-layouts  8.98 us (7%)
  matrix products  7.52 us (6%)
  other arithmetic  2.1 us (2%)
    all_to_all x2, blocking collectives, exchange(): lax.all_to_all(blocks, 'seq', split_axis=0, concat_axis=0, tiled=True)  29.3 us
    reduce_scatter x1, waiting for transfers between devices, local(): lax.psum_scatter(out_terms, 'seq', scatter_dimension=0, tiled=True)  29.1 us
    all_to_all x2, waiting for transfers between devices, exchange(): lax.all_to_all(blocks, 'seq', split_axis=0, concat_axis=0, tiled=True)  19.5 us
    all_to_all x2, starting transfers between devices, exchange(): lax.all_to_all(blocks, 'seq', split_axis=0, concat_axis=0, tiled=True)  10.9 us
    ppermute x1, waiting for transfers between devices, local(): other = lax.ppermute(share, 'dp', [(0, 1), (1, 0)])  7.72 us
    dot_general x8, matrix products, dot(): return lax.dot_general(a, b, dims, preferred_element_type=jnp.float32)  7.12 us
    another operation x3, local copies, waits for them, and re-layouts, to_blocks(): x[0].reshape(own, n, per * heads, HEAD).swapaxes(0, 1)  3.34 us
  transfers between devices with their start and end apart: 5, of which 5 were waited for; matrix products, arithmetic and copies ran while one was open for 14% of the time, Pallas kernels for 0%

profile of v2, /device:TPU:0, one launch (start us, length us, event | category | flops | bytes accessed | tf_op | source)
XLA Modules:
  0.0 134.1 jit_solution(8285697124992035007)
XLA Ops:
  7.2 0.7 all-gather.3.cloned.1.call-update
  7.9 1.1 reshape_transpose_reshape_squeeze.9
  9.0 1.1 reshape_transpose_reshape_squeeze.10
  10.2 1.1 reshape_transpose_reshape_squeeze.11
  11.3 0.8 pad_maximum_fusion
  12.1 7.4 %all-to-all-start = ((bf16[16,108,128]{2,1,0:T(8,128)(2,1)}), bf16[16,108,128]{2,1,0:T(8,128)(2,1)S(1)}, u32[]{:S(2)}, u32[]{:S(2)}) async-start(bf16[16,108,128]{2,1,0:T(8,128)(2,1)} %pad_maximum_fusion), calls=%async_computation | async-start | bytes 917504 | tf_op jit(solution)/shard_map/all_to_all | solution.py:15
  19.5 0.0 reduce-scatter.2.cloned.1.call-start
  19.6 0.1 broadcast_in_dim.19
  19.6 0.1 eq.38
  19.7 0.1 eq.42
  19.8 0.1 compare_and_fusion
  20.0 17.0 %all-to-all-done = bf16[16,108,128]{2,1,0:T(8,128)(2,1)S(1)} async-done(((bf16[16,108,128]{2,1,0:T(8,128)(2,1)}), bf16[16,108,128]{2,1,0:T(8,128)(2,1)S(1)}, u32[]{:S(2)}, u32[]{:S(2)}) %all-to-all-start) | async-done | bytes 442400 | tf_op jit(solution)/shard_map/all_to_all | solution.py:15
  36.9 0.1 fusion.15
  37.4 0.4 fusion.16
  37.8 0.6 convolution_convert_fusion.4
  38.5 0.2 reshape_reshape.6
  38.6 0.1 copy.63
  38.7 16.7 %all_to_all.20 = bf16[16,48,96]{2,1,0:T(8,128)(2,1)S(1)} all-to-all(bf16[16,48,96]{2,1,0:T(8,128)(2,1)S(1)} %copy.63), channel_id=1, replica_groups=mesh['dp'=2,'seq'=16] {'seq'}, dimensions={0} | all-to-all | bytes 294912 | tf_op jit(solution)/shard_map/all_to_all | solution.py:15
  55.4 0.1 copy.64
  55.5 0.1 copy.65
  55.6 0.2 reshape.148
  55.8 2.2 %convolution_convert_fusion = bf16[768,1536]{1,0:T(8,128)(2,1)} fusion(bf16[768,96]{1,0:T(8,128)(2,1)S(1)} %reshape.148, bf16[96,1536]{1,0:T(8,128)(2,1)S(1)} %copy-done), kind=kOutput, calls=%fused_computation.1 | convolution fusion | flops 227672064 | bytes 2801664 | tf_op jit(solution)/shard_map/dot_general | solution.py:11
  58.0 2.1 %all-gather.3.cloned.1.call-done = bf16[16,1,48,1536]{3,2,1,0:T(8,128)(2,1)} async-done(((bf16[1,1,48,1536]{3,2,1,0:T(8,128)(2,1)}), bf16[16,1,48,1536]{3,2,1,0:T(8,128)(2,1)}) %all-gather.3.cloned.1.call-update) | async-done | bytes 2359312 | tf_op jit(solution)/shard_map/all_gather | solution.py:44
  60.1 2.5 %convolution_convert_fusion.3 = bf16[768,96]{0,1:T(8,128)(2,1)S(1)} fusion(bf16[768,1536]{1,0:T(8,128)(2,1)} %bitcast.53, bf16[96,1536]{1,0:T(8,128)(2,1)S(1)} %copy-done), kind=kOutput, calls=%fused_computation.15 | convolution fusion | flops 226566144 | bytes 2801664 | tf_op jit(solution)/shard_map/dot_general | solution.py:11
  62.6 0.2 copy.66
  62.8 0.1 reshape.151
  63.0 0.1 copy.68
  63.0 12.6 %all_to_all.21 = bf16[16,48,96]{2,1,0:T(8,128)(2,1)S(1)} all-to-all(bf16[16,48,96]{2,1,0:T(8,128)(2,1)S(1)} %copy.68), channel_id=1, replica_groups=mesh['dp'=2,'seq'=16] {'seq'}, dimensions={0} | all-to-all | bytes 294912 | tf_op jit(solution)/shard_map/all_to_all | solution.py:15
  75.6 0.1 copy.69
  75.7 0.2 reshape_reshape.7
  75.9 0.2 multiply_reduce_fusion
  76.1 0.3 fusion.5
  76.4 0.2 fusion.7
  76.7 0.3 fusion.6
  77.1 0.5 convolution_convert_fusion.2
  77.7 0.1 pad_maximum_fusion.1
  77.8 0.9 copy.76
  78.7 3.6 %all-to-all-start.3 = ((bf16[16,108,128]{2,1,0:T(8,128)(2,1)}), bf16[16,108,128]{2,1,0:T(8,128)(2,1)S(1)}, u32[]{:S(2)}, u32[]{:S(2)}) async-start(bf16[16,108,128]{2,1,0:T(8,128)(2,1)} %copy.76), calls=%async_computation.4 | async-start | bytes 917504 | tf_op jit(solution)/shard_map/all_to_all | solution.py:15
  82.3 0.5 convolution_convert_fusion.1
  82.8 1.5 %collective-permute-start = (bf16[96,1536]{1,0:T(8,128)(2,1)S(1)}, bf16[96,1536]{1,0:T(8,128)(2,1)S(1)}, u32[]{:S(2)}, u32[]{:S(2)}) collective-permute-start(bf16[96,1536]{1,0:T(8,128)(2,1)S(1)} %convolution_convert_fusion.1), channel_id=1, source_target_pairs={{0,16},{16,0},{1,17},{17,1},{2,18},{18,2},{3,19},{19,3},{4,20},{20... | collective-permute-start | bytes 884744 | tf_op jit(solution)/shard_map/ppermute | solution.py:101
  84.4 7.7 %collective-permute-done = bf16[96,1536]{1,0:T(8,128)(2,1)S(1)} collective-permute-done((bf16[96,1536]{1,0:T(8,128)(2,1)S(1)}, bf16[96,1536]{1,0:T(8,128)(2,1)S(1)}, u32[]{:S(2)}, u32[]{:S(2)}) %collective-permute-start) | collective-permute-done | bytes 294944 | tf_op jit(solution)/shard_map/ppermute | solution.py:101
  92.1 0.9 convert_add_fusion
  93.0 2.5 %all-to-all-done.3 = bf16[16,108,128]{2,1,0:T(8,128)(2,1)S(1)} async-done(((bf16[16,108,128]{2,1,0:T(8,128)(2,1)}), bf16[16,108,128]{2,1,0:T(8,128)(2,1)S(1)}, u32[]{:S(2)}, u32[]{:S(2)}) %all-to-all-start.3) | async-done | bytes 442400 | tf_op jit(solution)/shard_map/all_to_all | solution.py:15
  95.5 0.1 fusion.14
  95.6 0.9 reshape_transpose_reshape.11
  96.4 0.9 reshape_transpose_reshape.10
  97.3 0.9 reshape_transpose_reshape.9
  98.1 29.1 %reduce-scatter.2.cloned.1.call-done = bf16[48,1536]{1,0:T(8,128)(2,1)} async-done(((bf16[768,1536]{1,0:T(8,128)(2,1)}), bf16[48,1536]{1,0:T(8,128)(2,1)}) %reduce-scatter.2.cloned.1.call-update) | async-done | bytes 147472 | tf_op jit(solution)/shard_map/reduce_scatter | solution.py:75
  (29 shorter events, 0.8 us)
Async XLA Ops:
  7.2 48.6 %copy-start = (bf16[96,1536]{1,0:T(8,128)(2,1)S(1)}, bf16[96,1536]{1,0:T(8,128)(2,1)}, u32[]{:S(2)}) copy-start(bf16[96,1536]{1,0:T(8,128)(2,1)} %param.10) | copy-start | bytes 884740
  7.2 12.4 %copy-start.2 = (s32[1,16]{1,0:T(1,128)S(1)}, s32[1,16]{1,0:T(1,128)}, u32[]{:S(2)}) copy-start(s32[1,16]{1,0:T(1,128)} %param.11) | copy-start | bytes 196
  7.2 52.9 %all-gather.3.cloned.1.call-start = ((), (), s32[]{:S(2)}) async-start(), calls=%async_computation.6 | async-start | bytes 2506752 | tf_op jit(solution)/shard_map/all_gather | solution.py:44
  12.1 24.8 %all-to-all-start = ((bf16[16,108,128]{2,1,0:T(8,128)(2,1)}), bf16[16,108,128]{2,1,0:T(8,128)(2,1)S(1)}, u32[]{:S(2)}, u32[]{:S(2)}) async-start(bf16[16,108,128]{2,1,0:T(8,128)(2,1)} %pad_maximum_fusion), calls=%async_computation | async-start | bytes 917504 | tf_op jit(solution)/shard_map/all_to_all | solution.py:15
  19.5 107.8 %reduce-scatter.2.cloned.1.call-start = ((), (), s32[]{:S(2)}) async-start(), calls=%async_computation.5 | async-start | bytes 2506752 | tf_op jit(solution)/shard_map/reduce_scatter | solution.py:75
  77.6 4.6 %copy-start.1 = (bf16[16,1,48,1536]{3,2,1,0:T(8,128)(2,1)S(1)}, bf16[16,1,48,1536]{3,2,1,0:T(8,128)(2,1)}, u32[]{:S(2)}) copy-start(bf16[16,1,48,1536]{3,2,1,0:T(8,128)(2,1)} %all-gather.3.cloned.1.call-done) | copy-start | bytes 7077892
  78.7 16.8 %all-to-all-start.3 = ((bf16[16,108,128]{2,1,0:T(8,128)(2,1)}), bf16[16,108,128]{2,1,0:T(8,128)(2,1)S(1)}, u32[]{:S(2)}, u32[]{:S(2)}) async-start(bf16[16,108,128]{2,1,0:T(8,128)(2,1)} %copy.76), calls=%async_computation.4 | async-start | bytes 917504 | tf_op jit(solution)/shard_map/all_to_all | solution.py:15
  82.8 9.3 %collective-permute-start = (bf16[96,1536]{1,0:T(8,128)(2,1)S(1)}, bf16[96,1536]{1,0:T(8,128)(2,1)S(1)}, u32[]{:S(2)}, u32[]{:S(2)}) collective-permute-start(bf16[96,1536]{1,0:T(8,128)(2,1)S(1)} %convolution_convert_fusion.1), channel_id=1, source_target_pairs={{0,16},{16,0},{1,17},{17,1},{2,18},{18,2},{3,19},{19,3},{4,20},{20... | collective-permute-start | bytes 884744 | tf_op jit(solution)/shard_map/ppermute | solution.py:101
Sparse Core Ops, SparseCore 0:
  10.3 49.7 all-gather.2
  64.4 62.7 reduce-scatter.1

commit v3 on v2

--- a/solution.py
+++ b/solution.py
@@ -71,11 +71,32 @@
         .reshape(frames * span, part)
     )
 
-    out_terms = dot(mixed_part, out_weight, (((1,), (0,)), ((), ()))).astype(LOW)
-    mixed_out = lax.psum_scatter(out_terms, "seq", scatter_dimension=0, tiled=True)
-    _, grad_all = lax.optimization_barrier((out_terms, grad_all))
+    place = lax.axis_index("seq")
+    pairs = mixed_part.reshape(n // 2, 2, own * span, part)
 
+    def terms(side):
+        picked = lax.dynamic_index_in_dim(pairs, side, 1, keepdims=False)
+        return dot(picked, out_weight, (((2,), (0,)), ((), ())))
+
+    sent = terms(1 - place % 2).astype(LOW)
+    _, grad_all = lax.optimization_barrier((sent, grad_all))
+    total = terms(place % 2) + lax.ppermute(
+        sent, "seq", [(i, i ^ 1) for i in range(n)]
+    ).astype(jnp.float32)
     mixed_grad = dot(grad_all, out_weight, (((1,), (1,)), ((), ()))).astype(LOW)
+    total, mixed_grad = lax.optimization_barrier((total, mixed_grad))
+    step = 2
+    while step < n:
+        halves = total.astype(LOW).reshape(n // step // 2, 2, own * span, total.shape[2])
+        side = (place // step) % 2
+        sent = lax.dynamic_index_in_dim(halves, 1 - side, 1, keepdims=False)
+        kept = lax.dynamic_index_in_dim(halves, side, 1, keepdims=False)
+        total = kept.astype(jnp.float32) + lax.ppermute(
+            sent, "seq", [(i, i ^ step) for i in range(n)]
+        ).astype(jnp.float32)
+        step = 2 * step
+    mixed_out = total.astype(LOW)
+
     mixed_grad = (
         mixed_grad.reshape(frames, n, per, part).swapaxes(0, 1).reshape(n, frames * per, part)
     )

time: 135 us -> 130 us (0.963)
  blocking collectives: 29.3 us -> 0 us
  starting transfers between devices: 12.6 us -> 29.9 us
  matrix products: 7.52 us -> 11.3 us
  other arithmetic: 2.1 us -> 5.03 us
  local copies, waits for them, and re-layouts: 8.98 us -> 11.5 us
  waiting for transfers between devices: 59.2 us -> 57.1 us
    all_to_all x2 -> x0, blocking collectives: 29.3 us -> none  [exchange(): lax.all_to_all(blocks, 'seq', split_axis=0, concat_axis=0, tiled=True)]
    reduce_scatter x1 -> x0, waiting for transfers between devices: 29.1 us -> none  [local(): lax.psum_scatter(out_terms, 'seq', scatter_dimension=0, tiled=True)]
    ppermute x0 -> x4, waiting for transfers between devices: none -> 24 us  [the longest x3 21.8 us: local(): lax.ppermute(sent, 'seq', [(i, i ^ step) for i in range(n)])]
    all_to_all x2 -> x4, waiting for transfers between devices: 19.5 us -> 32.4 us  [exchange(): lax.all_to_all(blocks, 'seq', split_axis=0, concat_axis=0, tiled=True)]
    all_to_all x2 -> x4, starting transfers between devices: 10.9 us -> 21.2 us  [exchange(): lax.all_to_all(blocks, 'seq', split_axis=0, concat_axis=0, tiled=True)]
    ppermute x1, waiting for transfers between devices: 7.72 us -> 0.01 us  [local(): other = lax.ppermute(share, 'dp', [(0, 1), (1, 0)])]
    ppermute x0 -> x4, starting transfers between devices: none -> 7.02 us  [the longest x3 6.41 us: local(): lax.ppermute(sent, 'seq', [(i, i ^ step) for i in range(n)])]
    dot_general x8 -> x9, matrix products: 7.12 us -> 10.1 us  [dot(): return lax.dot_general(a, b, dims, preferred_element_type=jnp.float32)]
  transfers between devices with their start and end apart: 5 -> 10, of which waited for: 5 -> 7; matrix products, arithmetic and copies ran while one was open for 14% -> 16% of each run, Pallas kernels for 0% -> 0%
where the time goes in v3:
time: 130 us; the launch traced here: 129 us
  waiting for transfers between devices  57.1 us (44%)
  starting transfers between devices  29.9 us (23%)
  between operations  14.6 us (11%)
  local copies, waits for them, and re-layouts  11.5 us (9%)
  matrix products  11.3 us (9%)
  other arithmetic  5.03 us (4%)
    all_to_all x4, waiting for transfers between devices, exchange(): lax.all_to_all(blocks, 'seq', split_axis=0, concat_axis=0, tiled=True)  32.4 us
    ppermute x3, waiting for transfers between devices, local(): lax.ppermute(sent, 'seq', [(i, i ^ step) for i in range(n)])  21.8 us
    all_to_all x4, starting transfers between devices, exchange(): lax.all_to_all(blocks, 'seq', split_axis=0, concat_axis=0, tiled=True)  21.2 us
    dot_general x9, matrix products, dot(): return lax.dot_general(a, b, dims, preferred_element_type=jnp.float32)  10.1 us
    ppermute x3, starting transfers between devices, local(): lax.ppermute(sent, 'seq', [(i, i ^ step) for i in range(n)])  6.41 us
    another operation x3, local copies, waits for them, and re-layouts, to_blocks(): x[0].reshape(own, n, per * heads, HEAD).swapaxes(0, 1)  3.34 us
  transfers between devices with their start and end apart: 10, of which 7 were waited for; matrix products, arithmetic and copies ran while one was open for 16% of the time, Pallas kernels for 0%

profile of v3, /device:TPU:0, one launch (start us, length us, event | category | flops | bytes accessed | tf_op | source)
XLA Modules:
  0.0 129.4 jit_solution(16334363679174555086)
XLA Ops:
  7.2 0.7 all-gather.3.cloned.1.call-update
  7.9 1.1 reshape_transpose_reshape_squeeze.9
  9.0 1.1 reshape_transpose_reshape_squeeze.10
  10.2 1.1 reshape_transpose_reshape_squeeze.11
  11.3 0.8 pad_maximum_fusion
  12.1 7.4 %all-to-all-start = ((bf16[16,108,128]{2,1,0:T(8,128)(2,1)}), bf16[16,108,128]{2,1,0:T(8,128)(2,1)S(1)}, u32[]{:S(2)}, u32[]{:S(2)}) async-start(bf16[16,108,128]{2,1,0:T(8,128)(2,1)} %pad_maximum_fusion), calls=%async_computation | async-start | bytes 917504 | tf_op jit(solution)/shard_map/all_to_all | solution.py:15
  19.9 17.0 %all-to-all-done = bf16[16,108,128]{2,1,0:T(8,128)(2,1)S(1)} async-done(((bf16[16,108,128]{2,1,0:T(8,128)(2,1)}), bf16[16,108,128]{2,1,0:T(8,128)(2,1)S(1)}, u32[]{:S(2)}, u32[]{:S(2)}) %all-to-all-start) | async-done | bytes 442400 | tf_op jit(solution)/shard_map/all_to_all | solution.py:15
  37.4 1.2 fusion.28
  38.6 0.6 convolution_convert_fusion.4
  39.3 0.6 copy-done.4
  39.9 0.2 reshape_reshape.9
  40.1 0.7 copy.70
  40.8 4.5 %all-to-all-start.1 = ((bf16[16,48,96]{2,1,0:T(8,128)(2,1)}), bf16[16,48,96]{2,1,0:T(8,128)(2,1)S(1)}, u32[]{:S(2)}, u32[]{:S(2)}) async-start(bf16[16,48,96]{2,1,0:T(8,128)(2,1)} %copy.70), calls=%async_computation.1 | async-start | bytes 393216 | tf_op jit(solution)/shard_map/all_to_all | solution.py:15
  45.3 10.6 %all-to-all-done.1 = bf16[16,48,96]{2,1,0:T(8,128)(2,1)S(1)} async-done(((bf16[16,48,96]{2,1,0:T(8,128)(2,1)}), bf16[16,48,96]{2,1,0:T(8,128)(2,1)S(1)}, u32[]{:S(2)}, u32[]{:S(2)}) %all-to-all-start.1) | async-done | bytes 147488 | tf_op jit(solution)/shard_map/all_to_all | solution.py:15
  56.1 0.4 constant_dynamic-slice_fusion.2
  56.5 0.4 convolution_convert_fusion
  57.0 0.6 collective-permute-start
  57.7 0.2 reshape.178
  57.9 2.2 %collective-permute-done = bf16[8,48,1536]{2,1,0:T(8,128)(2,1)S(1)} collective-permute-done((bf16[8,48,1536]{2,1,0:T(8,128)(2,1)S(1)}, bf16[8,48,1536]{2,1,0:T(8,128)(2,1)S(1)}, u32[]{:S(2)}, u32[]{:S(2)}) %collective-permute-start) | collective-permute-done | bytes 1179680 | tf_op jit(solution)/shard_map/ppermute | solution.py:83
  60.1 1.5 %convert_add_fusion = bf16[8,48,1536]{2,1,0:T(8,128)(2,1)} fusion(bf16[8,48,1536]{2,1,0:T(8,128)(2,1)S(1)} %collective-permute-done, bf16[96,1536]{1,0:T(8,128)(2,1)S(1)} %copy-done, bf16[8,1,48,96]{3,1,0,2:T(2,128)(2,1)S(1)} %get-tuple-element.17), kind=kOutput, calls=%fused_computation.2 | convolution fusion | flops 115015680 | bytes 2727936 | tf_op jit(solution)/shard_map/dot_general | solution.py:11
  61.5 2.6 %convolution_convert_fusion.3 = bf16[768,96]{0,1:T(8,128)(2,1)S(1)} fusion(bf16[768,1536]{1,0:T(8,128)(2,1)} %bitcast.80, bf16[96,1536]{1,0:T(8,128)(2,1)S(1)} %copy-done), kind=kOutput, calls=%fused_computation.18 | convolution fusion | flops 226566144 | bytes 2801664 | tf_op jit(solution)/shard_map/dot_general | solution.py:11
  64.2 0.2 copy.76
  64.4 0.1 reshape.169
  64.6 0.7 copy.78
  65.3 5.3 %all-to-all-start.2 = ((bf16[16,48,96]{2,1,0:T(8,128)(2,1)}), bf16[16,48,96]{2,1,0:T(8,128)(2,1)S(1)}, u32[]{:S(2)}, u32[]{:S(2)}) async-start(bf16[16,48,96]{2,1,0:T(8,128)(2,1)} %copy.78), calls=%async_computation.2 | async-start | bytes 393216 | tf_op jit(solution)/shard_map/all_to_all | solution.py:15
  70.7 0.5 convolution_convert_fusion.1
  71.2 1.6 %collective-permute-start.4 = (bf16[96,1536]{1,0:T(8,128)(2,1)S(1)}, bf16[96,1536]{1,0:T(8,128)(2,1)}, u32[]{:S(2)}, u32[]{:S(2)}) collective-permute-start(bf16[96,1536]{1,0:T(8,128)(2,1)S(1)} %convolution_convert_fusion.1), channel_id=1, source_target_pairs={{0,16},{16,0},{1,17},{17,1},{2,18},{18,2},{3,19},{19,3},{4,20},{20... | collective-permute-start | bytes 884744 | tf_op jit(solution)/shard_map/ppermute | solution.py:122
  72.9 2.0 %collective-permute-start.1 = (bf16[4,48,1536]{2,1,0:T(8,128)(2,1)S(1)}, bf16[4,48,1536]{2,1,0:T(8,128)(2,1)}, u32[]{:S(2)}, u32[]{:S(2)}) collective-permute-start(bf16[4,48,1536]{2,1,0:T(8,128)(2,1)S(1)} %dynamic-slice_bitcast_fusion), channel_id=1, source_target_pairs={{0,2},{1,3},{2,0},{3,1},{4,6},{5,7},{6,4},{7,5},{8,10},{9,11},{10,... | collective-permute-start | bytes 1769480 | tf_op jit(solution)/shard_map/ppermute | solution.py:94
  74.9 4.8 %all-to-all-done.2 = bf16[16,48,96]{2,1,0:T(8,128)(2,1)S(1)} async-done(((bf16[16,48,96]{2,1,0:T(8,128)(2,1)}), bf16[16,48,96]{2,1,0:T(8,128)(2,1)S(1)}, u32[]{:S(2)}, u32[]{:S(2)}) %all-to-all-start.2) | async-done | bytes 147488 | tf_op jit(solution)/shard_map/all_to_all | solution.py:15
  79.7 0.2 reshape_reshape.11
  80.0 0.2 multiply_reduce_fusion
  80.2 1.4 %fusion.5 = bf16[3,192,192]{1,2,0:T(8,128)(2,1)S(1)} fusion(bf16[3,192,128]{2,1,0:T(8,128)(2,1)S(1)} %reshape.171, bf16[3,192,128]{2,1,0:T(8,128)(2,1)S(1)} %copy-done.10, f32[3,192]{1,0:T(4,128)S(1)} %multiply_reduce_fusion, f32[3,192,192]{1,2,0:T(8,128)} %get-tuple-element.20, f32[3,192]{1,0:T(4,128)S(1)} %copy-done.13), kind=kOutput, calls=%fused_computation.10 | convolution fusion | flops 28753920 | bytes 963072 | tf_op jit(solution)/shard_map/dot_general | solution.py:11
  81.6 0.2 fusion.8
  81.9 1.2 fusion.7
  83.3 6.2 %collective-permute-done.1 = bf16[4,48,1536]{2,1,0:T(8,128)(2,1)} collective-permute-done((bf16[4,48,1536]{2,1,0:T(8,128)(2,1)S(1)}, bf16[4,48,1536]{2,1,0:T(8,128)(2,1)}, u32[]{:S(2)}, u32[]{:S(2)}) %collective-permute-start.1) | collective-permute-done | bytes 589856 | tf_op jit(solution)/shard_map/ppermute | solution.py:94
  89.5 1.2 fusion.6
  90.7 1.8 %collective-permute-start.2 = (bf16[2,48,1536]{2,1,0:T(8,128)(2,1)S(1)}, bf16[2,48,1536]{2,1,0:T(8,128)(2,1)S(1)}, u32[]{:S(2)}, u32[]{:S(2)}) collective-permute-start(bf16[2,48,1536]{2,1,0:T(8,128)(2,1)S(1)} %dynamic-slice_bitcast_fusion.1), channel_id=1, source_target_pairs={{0,4},{1,5},{2,6},{3,7},{4,0},{5,1},{6,2},{7,3},{8,12},{9,13},{10,... | collective-permute-start | bytes 884744 | tf_op jit(solution)/shard_map/ppermute | solution.py:94
  92.5 1.5 %convolution_convert_fusion.2 = bf16[3,192,128]{2,1,0:T(8,128)(2,1)S(1)} fusion(bf16[3,192,128]{2,1,0:T(8,128)(2,1)S(1)} %reshape.171, f32[3,192]{1,0:T(4,128)S(1)} %copy-done.13, bf16[3,192,128]{2,1,0:T(8,128)(2,1)} %copy-done.7, bf16[3,192,128]{2,1,0:T(8,128)(2,1)} %copy-done.6, pred[192,192]{0,1:T(8,128)(4,1)S(1)} %compare_and_fusion), kind=kOutput, calls=%fused_computation.17 | convolution fusion | flops 57250560 | bytes 628992 | tf_op jit(solution)/shard_map/dot_general | solution.py:11
  94.1 0.9 copy.86
  95.0 4.1 %all-to-all-start.3 = ((bf16[16,108,128]{2,1,0:T(8,128)(2,1)}), bf16[16,108,128]{2,1,0:T(8,128)(2,1)S(1)}, u32[]{:S(2)}, u32[]{:S(2)}) async-start(bf16[16,108,128]{2,1,0:T(8,128)(2,1)} %copy.86), calls=%async_computation.3 | async-start | bytes 917504 | tf_op jit(solution)/shard_map/all_to_all | solution.py:15
  99.1 0.3 collective-permute-done.2
  99.5 2.6 %collective-permute-start.3 = (bf16[1,48,1536]{2,1,0:T(8,128)(2,1)S(1)}, bf16[1,48,1536]{2,1,0:T(8,128)(2,1)S(1)}, u32[]{:S(2)}, u32[]{:S(2)}) collective-permute-start(bf16[1,48,1536]{2,1,0:T(8,128)(2,1)S(1)} %constant_dynamic-slice_fusion), channel_id=1, source_target_pairs={{0,8},{1,9},{2,10},{3,11},{4,12},{5,13},{6,14},{7,15},{8,0},{9,1},... | collective-permute-start | bytes 442376 | tf_op jit(solution)/shard_map/ppermute | solution.py:94
  102.1 1.8 %convert_add_fusion.3 = f32[96,1536]{1,0:T(8,128)} fusion(bf16[96,1536]{1,0:T(8,128)(2,1)} %collective-permute-done.4, bf16[96,1536]{1,0:T(8,128)(2,1)S(1)} %convolution_convert_fusion.1), kind=kLoop, calls=%fused_computation.22 | loop fusion | flops 442368 | bytes 1179648 | tf_op jit(solution)/shard_map/add | solution.py:123
  104.0 15.3 %collective-permute-done.3 = bf16[1,48,1536]{2,1,0:T(8,128)(2,1)S(1)} collective-permute-done((bf16[1,48,1536]{2,1,0:T(8,128)(2,1)S(1)}, bf16[1,48,1536]{2,1,0:T(8,128)(2,1)S(1)}, u32[]{:S(2)}, u32[]{:S(2)}) %collective-permute-start.3) | collective-permute-done | bytes 147488 | tf_op jit(solution)/shard_map/ppermute | solution.py:94
  119.3 0.7 fusion.16
  120.0 0.9 reshape_transpose_reshape.11
  120.9 0.9 reshape_transpose_reshape.10
  121.7 0.9 reshape_transpose_reshape.9
  (67 shorter events, 1.8 us)
Async XLA Ops:
  7.2 49.3 %copy-start = (bf16[96,1536]{1,0:T(8,128)(2,1)S(1)}, bf16[96,1536]{1,0:T(8,128)(2,1)}, u32[]{:S(2)}) copy-start(bf16[96,1536]{1,0:T(8,128)(2,1)} %param.10) | copy-start | bytes 884740
  7.2 12.3 %copy-start.11 = (s32[1,16]{1,0:T(1,128)S(1)}, s32[1,16]{1,0:T(1,128)}, u32[]{:S(2)}) copy-start(s32[1,16]{1,0:T(1,128)} %param.11) | copy-start | bytes 196
  7.2 54.4 %all-gather.3.cloned.1.call-start = ((), (), s32[]{:S(2)}) async-start(), calls=%async_computation.4 | async-start | bytes 2506752 | tf_op jit(solution)/shard_map/all_gather | solution.py:44
  12.1 24.8 %all-to-all-start = ((bf16[16,108,128]{2,1,0:T(8,128)(2,1)}), bf16[16,108,128]{2,1,0:T(8,128)(2,1)S(1)}, u32[]{:S(2)}, u32[]{:S(2)}) async-start(bf16[16,108,128]{2,1,0:T(8,128)(2,1)} %pad_maximum_fusion), calls=%async_computation | async-start | bytes 917504 | tf_op jit(solution)/shard_map/all_to_all | solution.py:15
  37.1 19.4 %copy-start.6 = (bf16[3,192,128]{2,1,0:T(8,128)(2,1)}, bf16[3,192,128]{2,1,0:T(8,128)(2,1)S(1)}, u32[]{:S(2)}) copy-start(bf16[3,192,128]{2,1,0:T(8,128)(2,1)S(1)} %reshape.160) | copy-start | bytes 442372
  37.3 2.0 %copy-start.9 = (bf16[3,192,128]{2,1,0:T(8,128)(2,1)}, bf16[3,192,128]{2,1,0:T(8,128)(2,1)S(1)}, u32[]{:S(2)}) copy-start(bf16[3,192,128]{2,1,0:T(8,128)(2,1)S(1)} %reshape.162) | copy-start | bytes 442372
  37.4 1.2 copy-start.7
  38.6 1.3 copy-start.12
  39.2 0.7 copy-start.4
  40.8 15.1 %all-to-all-start.1 = ((bf16[16,48,96]{2,1,0:T(8,128)(2,1)}), bf16[16,48,96]{2,1,0:T(8,128)(2,1)S(1)}, u32[]{:S(2)}, u32[]{:S(2)}) async-start(bf16[16,48,96]{2,1,0:T(8,128)(2,1)} %copy.70), calls=%async_computation.1 | async-start | bytes 393216 | tf_op jit(solution)/shard_map/all_to_all | solution.py:15
  57.0 3.1 %collective-permute-start = (bf16[8,48,1536]{2,1,0:T(8,128)(2,1)S(1)}, bf16[8,48,1536]{2,1,0:T(8,128)(2,1)S(1)}, u32[]{:S(2)}, u32[]{:S(2)}) collective-permute-start(bf16[8,48,1536]{2,1,0:T(8,128)(2,1)S(1)} %convolution_convert_fusion), channel_id=1, source_target_pairs={{0,1},{1,0},{2,3},{3,2},{4,5},{5,4},{6,7},{7,6},{8,9},{9,8},{10,11... | collective-permute-start | bytes 3538952 | tf_op jit(solution)/shard_map/ppermute | solution.py:83
  61.5 9.1 %copy-start.1 = (bf16[16,1,48,1536]{3,2,1,0:T(8,128)(2,1)S(1)}, bf16[16,1,48,1536]{3,2,1,0:T(8,128)(2,1)}, u32[]{:S(2)}) copy-start(bf16[16,1,48,1536]{3,2,1,0:T(8,128)(2,1)} %all-gather.3.cloned.1.call-done) | copy-start | bytes 7077892
  65.3 14.4 %all-to-all-start.2 = ((bf16[16,48,96]{2,1,0:T(8,128)(2,1)}), bf16[16,48,96]{2,1,0:T(8,128)(2,1)S(1)}, u32[]{:S(2)}, u32[]{:S(2)}) async-start(bf16[16,48,96]{2,1,0:T(8,128)(2,1)} %copy.78), calls=%async_computation.2 | async-start | bytes 393216 | tf_op jit(solution)/shard_map/all_to_all | solution.py:15
  70.6 2.2 %copy-start.2 = (bf16[8,48,1536]{2,1,0:T(8,128)(2,1)S(1)}, bf16[8,48,1536]{2,1,0:T(8,128)(2,1)}, u32[]{:S(2)}) copy-start(bf16[8,48,1536]{2,1,0:T(8,128)(2,1)} %convert_add_fusion) | copy-start | bytes 3538948
  70.7 9.5 %copy-start.13 = (f32[3,192]{1,0:T(4,128)S(1)}, f32[3,192]{1,0:T(4,128)}, u32[]{:S(2)}) copy-start(f32[3,192]{1,0:T(4,128)} %copy-done.12) | copy-start | bytes 6916
  71.2 8.7 %copy-start.5 = (bf16[3,192,128]{2,1,0:T(8,128)(2,1)S(1)}, bf16[3,192,128]{2,1,0:T(8,128)(2,1)}, u32[]{:S(2)}) copy-start(bf16[3,192,128]{2,1,0:T(8,128)(2,1)} %copy-done.4) | copy-start | bytes 442372
  71.2 8.9 %copy-start.10 = (bf16[3,192,128]{2,1,0:T(8,128)(2,1)S(1)}, bf16[3,192,128]{2,1,0:T(8,128)(2,1)}, u32[]{:S(2)}) copy-start(bf16[3,192,128]{2,1,0:T(8,128)(2,1)} %copy-done.9) | copy-start | bytes 442372
  71.2 30.9 %collective-permute-start.4 = (bf16[96,1536]{1,0:T(8,128)(2,1)S(1)}, bf16[96,1536]{1,0:T(8,128)(2,1)}, u32[]{:S(2)}, u32[]{:S(2)}) collective-permute-start(bf16[96,1536]{1,0:T(8,128)(2,1)S(1)} %convolution_convert_fusion.1), channel_id=1, source_target_pairs={{0,16},{16,0},{1,17},{17,1},{2,18},{18,2},{3,19},{19,3},{4,20},{20... | collective-permute-start | bytes 884744 | tf_op jit(solution)/shard_map/ppermute | solution.py:122
  72.9 8.7 %copy-start.8 = (bf16[3,192,128]{2,1,0:T(8,128)(2,1)S(1)}, bf16[3,192,128]{2,1,0:T(8,128)(2,1)}, u32[]{:S(2)}) copy-start(bf16[3,192,128]{2,1,0:T(8,128)(2,1)} %copy-done.7) | copy-start | bytes 442372
  72.9 16.6 %collective-permute-start.1 = (bf16[4,48,1536]{2,1,0:T(8,128)(2,1)S(1)}, bf16[4,48,1536]{2,1,0:T(8,128)(2,1)}, u32[]{:S(2)}, u32[]{:S(2)}) collective-permute-start(bf16[4,48,1536]{2,1,0:T(8,128)(2,1)S(1)} %dynamic-slice_bitcast_fusion), channel_id=1, source_target_pairs={{0,2},{1,3},{2,0},{3,1},{4,6},{5,7},{6,4},{7,5},{8,10},{9,11},{10,... | collective-permute-start | bytes 1769480 | tf_op jit(solution)/shard_map/ppermute | solution.py:94
  80.2 9.3 %copy-start.3 = (bf16[8,48,1536]{2,1,0:T(8,128)(2,1)S(1)}, bf16[8,48,1536]{2,1,0:T(8,128)(2,1)}, u32[]{:S(2)}) copy-start(bf16[8,48,1536]{2,1,0:T(8,128)(2,1)} %convert_add_fusion) | copy-start | bytes 3538948
  90.7 8.7 %collective-permute-start.2 = (bf16[2,48,1536]{2,1,0:T(8,128)(2,1)S(1)}, bf16[2,48,1536]{2,1,0:T(8,128)(2,1)S(1)}, u32[]{:S(2)}, u32[]{:S(2)}) collective-permute-start(bf16[2,48,1536]{2,1,0:T(8,128)(2,1)S(1)} %dynamic-slice_bitcast_fusion.1), channel_id=1, source_target_pairs={{0,4},{1,5},{2,6},{3,7},{4,0},{5,1},{6,2},{7,3},{8,12},{9,13},{10,... | collective-permute-start | bytes 884744 | tf_op jit(solution)/shard_map/ppermute | solution.py:94
  95.0 24.9 %all-to-all-start.3 = ((bf16[16,108,128]{2,1,0:T(8,128)(2,1)}), bf16[16,108,128]{2,1,0:T(8,128)(2,1)S(1)}, u32[]{:S(2)}, u32[]{:S(2)}) async-start(bf16[16,108,128]{2,1,0:T(8,128)(2,1)} %copy.86), calls=%async_computation.3 | async-start | bytes 917504 | tf_op jit(solution)/shard_map/all_to_all | solution.py:15
  99.5 19.8 %collective-permute-start.3 = (bf16[1,48,1536]{2,1,0:T(8,128)(2,1)S(1)}, bf16[1,48,1536]{2,1,0:T(8,128)(2,1)S(1)}, u32[]{:S(2)}, u32[]{:S(2)}) collective-permute-start(bf16[1,48,1536]{2,1,0:T(8,128)(2,1)S(1)} %constant_dynamic-slice_fusion), channel_id=1, source_target_pairs={{0,8},{1,9},{2,10},{3,11},{4,12},{5,13},{6,14},{7,15},{8,0},{9,1},... | collective-permute-start | bytes 442376 | tf_op jit(solution)/shard_map/ppermute | solution.py:94
Sparse Core Ops, SparseCore 0:
  10.3 50.4 all-gather.2

commit v4 on v3

--- a/solution.py
+++ b/solution.py
@@ -1,6 +1,10 @@
+import functools
+
 import jax
 import jax.numpy as jnp
 from jax import lax
+from jax.experimental import pallas as pl
+from jax.experimental.pallas import tpu as pltpu
 from jax.sharding import PartitionSpec as P
 
 HEAD = 128
@@ -11,8 +15,73 @@
     return lax.dot_general(a, b, dims, preferred_element_type=jnp.float32)
 
 
-def exchange(blocks):
-    return lax.all_to_all(blocks, "seq", split_axis=0, concat_axis=0, tiled=True)
+def exchange_kernel(n, x_ref, o_ref, send_sem, recv_sem, own_sem):
+    me = lax.axis_index("seq")
+    replica = lax.axis_index("dp")
+
+    def peer(k):
+        return lax.rem(me + k, n)
+
+    barrier = pltpu.get_barrier_semaphore()
+
+    def greet(k, carry):
+        pl.semaphore_signal(
+            barrier, inc=1, device_id=(replica, peer(k)), device_id_type=pl.DeviceIdType.MESH
+        )
+        return carry
+
+    lax.fori_loop(1, n, greet, 0)
+    pl.semaphore_wait(barrier, n - 1)
+
+    def copy(k):
+        return pltpu.make_async_remote_copy(
+            src_ref=x_ref.at[peer(k)],
+            dst_ref=o_ref.at[me],
+            send_sem=send_sem.at[k],
+            recv_sem=recv_sem.at[k],
+            device_id=(replica, peer(k)),
+            device_id_type=pl.DeviceIdType.MESH,
+        )
+
+    def begin(k, carry):
+        copy(k).start()
+        return carry
+
+    def finish(k, carry):
+        copy(k).wait()
+        return carry
+
+    lax.fori_loop(1, n, begin, 0)
+    own = pltpu.make_async_copy(x_ref.at[me], o_ref.at[me], own_sem)
+    own.start()
+    own.wait()
+    lax.fori_loop(1, n, finish, 0)
+
+
+def exchange(blocks, which):
+    n, rows, lanes = blocks.shape
+    full_rows, full_lanes = -(-rows // 16) * 16, -(-lanes // 128) * 128
+    blocks = jnp.pad(blocks, ((0, 0), (0, full_rows - rows), (0, full_lanes - lanes)))
+    size = 2 * n * full_rows * full_lanes
+    moved = pl.pallas_call(
+        functools.partial(exchange_kernel, n),
+        out_shape=jax.ShapeDtypeStruct(blocks.shape, blocks.dtype),
+        in_specs=[pl.BlockSpec(memory_space=pltpu.VMEM)],
+        out_specs=pl.BlockSpec(memory_space=pltpu.VMEM),
+        scratch_shapes=[
+            pltpu.SemaphoreType.DMA((n,)),
+            pltpu.SemaphoreType.DMA((n,)),
+            pltpu.SemaphoreType.DMA,
+        ],
+        compiler_params=pltpu.CompilerParams(
+            collective_id=which, has_side_effects=True, vmem_limit_bytes=16 * 1024 * 1024
+        ),
+        cost_estimate=pl.CostEstimate(
+            flops=0, bytes_accessed=64 * size, transcendentals=0
+        ),
+        name="exchange",
+    )(blocks)
+    return moved[:, :rows, :lanes]
 
 
 def local(queries, key_field, value_field, out_grad, out_weight, frame_video):
@@ -45,7 +114,7 @@
     grad_all = grad_all.reshape(frames * span, out_grad.shape[3])
 
     spread = exchange(
-        jnp.concatenate([to_blocks(x) for x in (queries, key_field, value_field)], axis=1)
+        jnp.concatenate([to_blocks(x) for x in (queries, key_field, value_field)], axis=1), 0
     )
     query, key, value = (
         to_places(spread[:, i * rows : (i + 1) * rows]) for i in range(3)
@@ -65,7 +134,7 @@
 
     by_feature = to_frames(mixed).reshape(frames * per, n, part).swapaxes(0, 1)
     mixed_part = (
-        exchange(by_feature)
+        exchange(by_feature, 1)
         .reshape(n, frames, per, part)
         .swapaxes(0, 1)
         .reshape(frames * span, part)
@@ -100,7 +169,7 @@
     mixed_grad = (
         mixed_grad.reshape(frames, n, per, part).swapaxes(0, 1).reshape(n, frames * per, part)
     )
-    grad = to_places(exchange(mixed_grad).swapaxes(0, 1).reshape(frames, per, width))
+    grad = to_places(exchange(mixed_grad, 2).swapaxes(0, 1).reshape(frames, per, width))
 
     value_grad = dot(probs_low, grad, across).astype(LOW)
     through = dot(grad, value, inside)
@@ -111,7 +180,7 @@
     query_grad = (dot(score_grad, key, onward) * factor).astype(LOW)
     key_grad = (dot(score_grad, query, across) * factor).astype(LOW)
     home = exchange(
-        jnp.concatenate([to_frames(x) for x in (query_grad, key_grad, value_grad)], axis=1)
+        jnp.concatenate([to_frames(x) for x in (query_grad, key_grad, value_grad)], axis=1), 3
     )
     q_back, k_back, v_back = (
         from_blocks(home[:, i * rows : (i + 1) * rows]) for i in range(3)

time: 130 us -> 128 us (0.985)
  Pallas kernels: 0 us -> 51.7 us
  waiting for transfers between devices: 57.1 us -> 28.6 us
  starting transfers between devices: 29.9 us -> 7.24 us
  matrix products: 11.3 us -> 9.97 us
    pallas_call x0 -> x4, Pallas kernels: none -> 51.7 us  [exchange(): pl.pallas_call(functools.partial(exchange_kernel, n), out_shape=jax.Shape...]
    all_to_all x4 -> x0, waiting for transfers between devices: 32.4 us -> none  [exchange(): lax.all_to_all(blocks, 'seq', split_axis=0, concat_axis=0, tiled=True)]
    all_to_all x4 -> x0, starting transfers between devices: 21.2 us -> none  [exchange(): lax.all_to_all(blocks, 'seq', split_axis=0, concat_axis=0, tiled=True)]
    all_gather x1, waiting for transfers between devices: 0.01 us -> 8.75 us  [local(): grad_all = lax.all_gather(out_grad[0], 'seq', axis=0, tiled=True)]
    ppermute x3, waiting for transfers between devices: 21.8 us -> 16.7 us  [local(): lax.ppermute(sent, 'seq', [(i, i ^ step) for i in range(n)])]
    dot_general x9, matrix products: 10.1 us -> 8.78 us  [dot(): return lax.dot_general(a, b, dims, preferred_element_type=jnp.float32)]
  transfers between devices with their start and end apart: 10 -> 6, of which waited for: 7 -> 4; matrix products, arithmetic and copies ran while one was open for 16% -> 16% of each run, Pallas kernels for 0% -> 41%
where the time goes in v4:
time: 128 us; the launch traced here: 127 us
  Pallas kernels  51.7 us (40%)
  waiting for transfers between devices  28.6 us (22%)
  between operations  14.7 us (11%)
  local copies, waits for them, and re-layouts  10.5 us (8%)
  matrix products  9.97 us (8%)
  starting transfers between devices  7.24 us (6%)
  other arithmetic  4.3 us (3%)
    pallas_call x4, Pallas kernels, exchange(): pl.pallas_call(functools.partial(exchange_kernel, n), out_shape=jax.Shape...  51.7 us
    ppermute x3, waiting for transfers between devices, local(): lax.ppermute(sent, 'seq', [(i, i ^ step) for i in range(n)])  16.7 us
    dot_general x9, matrix products, dot(): return lax.dot_general(a, b, dims, preferred_element_type=jnp.float32)  8.78 us
    all_gather x1, waiting for transfers between devices, local(): grad_all = lax.all_gather(out_grad[0], 'seq', axis=0, tiled=True)  8.75 us
    ppermute x3, starting transfers between devices, local(): lax.ppermute(sent, 'seq', [(i, i ^ step) for i in range(n)])  5.59 us
    another operation x3, local copies, waits for them, and re-layouts, to_blocks(): x[0].reshape(own, n, per * heads, HEAD).swapaxes(0, 1)  3.34 us
  transfers between devices with their start and end apart: 6, of which 4 were waited for; matrix products, arithmetic and copies ran while one was open for 16% of the time, Pallas kernels for 41%

profile of v4, /device:TPU:0, one launch (start us, length us, event | category | flops | bytes accessed | tf_op | source)
XLA Modules:
  0.0 127.1 jit_solution(11572004697528275751)
XLA Ops:
  7.2 0.7 all-gather.3.cloned.1.call-update
  7.9 0.7 broadcast_in_dim.19
  8.7 0.1 eq.44
  8.8 0.1 eq.48
  8.8 1.1 reshape_transpose_reshape_squeeze.9
  10.0 1.1 reshape_transpose_reshape_squeeze.10
  11.1 1.1 reshape_transpose_reshape_squeeze.11
  12.2 0.1 fusion.17.x_ref
  12.3 17.5 %exchange.4 = bf16[16,112,128]{2,1,0:T(8,128)(2,1)S(1)} custom-call(bf16[16,112,128]{2,1,0:T(8,128)(2,1)S(1)} %fusion.17.x_ref), custom_call_target="tpu_custom_call" | custom-call | bytes 29360128 | tf_op jit(solution)/shard_map/exchange/pallas_call | solution.py:66
  30.3 0.1 compare_and_fusion
  30.4 1.2 fusion.38
  31.6 0.6 convolution_convert_fusion.4
  32.3 0.2 reshape_reshape.9
  32.6 12.5 %exchange.5 = bf16[16,48,128]{2,1,0:T(8,128)(2,1)S(1)} custom-call(bf16[16,48,128]{2,1,0:T(8,128)(2,1)S(1)} %pad.15.x_ref), custom_call_target="tpu_custom_call" | custom-call | bytes 12582912 | tf_op jit(solution)/shard_map/exchange/pallas_call | solution.py:66
  45.3 1.1 constant_dynamic-slice_fusion.2
  46.4 0.4 convolution_convert_fusion
  47.0 0.1 copy.76
  47.1 0.2 reshape.178
  47.3 2.4 %collective-permute-done = bf16[8,48,1536]{2,1,0:T(8,128)(2,1)S(1)} collective-permute-done((bf16[8,48,1536]{2,1,0:T(8,128)(2,1)S(1)}, bf16[8,48,1536]{2,1,0:T(8,128)(2,1)S(1)}, u32[]{:S(2)}, u32[]{:S(2)}) %collective-permute-start) | collective-permute-done | bytes 1179680 | tf_op jit(solution)/shard_map/ppermute | solution.py:152
  49.7 1.4 %convert_add_fusion = bf16[8,48,1536]{2,1,0:T(8,128)(2,1)S(1)} fusion(bf16[8,48,1536]{2,1,0:T(8,128)(2,1)S(1)} %collective-permute-done, bf16[96,1536]{1,0:T(8,128)(2,1)S(1)} %copy-done, bf16[8,1,48,96]{3,1,0,2:T(2,128)(2,1)} %get-tuple-element.17), kind=kOutput, calls=%fused_computation.2 | convolution fusion | flops 115015680 | bytes 2727936 | tf_op jit(solution)/shard_map/dot_general | solution.py:15
  51.1 8.7 %all-gather.3.cloned.1.call-done = bf16[16,1,48,1536]{3,2,1,0:T(8,128)(2,1)} async-done(((bf16[1,1,48,1536]{3,2,1,0:T(8,128)(2,1)}), bf16[16,1,48,1536]{3,2,1,0:T(8,128)(2,1)}) %all-gather.3.cloned.1.call-update) | async-done | bytes 2359312 | tf_op jit(solution)/shard_map/all_gather | solution.py:113
  59.8 2.6 %convolution_convert_fusion.3 = bf16[768,96]{0,1:T(8,128)(2,1)S(1)} fusion(bf16[768,1536]{1,0:T(8,128)(2,1)} %bitcast.85, bf16[96,1536]{1,0:T(8,128)(2,1)S(1)} %copy-done), kind=kOutput, calls=%fused_computation.18 | convolution fusion | flops 226566144 | bytes 2801664 | tf_op jit(solution)/shard_map/dot_general | solution.py:15
  62.5 0.5 convolution_convert_fusion.1
  63.0 1.5 %collective-permute-start.4 = (bf16[96,1536]{1,0:T(8,128)(2,1)S(1)}, bf16[96,1536]{1,0:T(8,128)(2,1)}, u32[]{:S(2)}, u32[]{:S(2)}) collective-permute-start(bf16[96,1536]{1,0:T(8,128)(2,1)S(1)} %convolution_convert_fusion.1), channel_id=1, source_target_pairs={{0,16},{16,0},{1,17},{17,1},{2,18},{18,2},{3,19},{19,3},{4,20},{20... | collective-permute-start | bytes 884744 | tf_op jit(solution)/shard_map/ppermute | solution.py:191
  64.6 0.2 copy.63
  64.7 0.1 reshape.169
  65.1 7.2 %exchange.6 = bf16[16,48,128]{2,1,0:T(8,128)(2,1)S(1)} custom-call(bf16[16,48,128]{2,1,0:T(8,128)(2,1)S(1)} %pad.16.x_ref), custom_call_target="tpu_custom_call" | custom-call | bytes 12582912 | tf_op jit(solution)/shard_map/exchange/pallas_call | solution.py:66
  72.3 0.2 reshape_reshape.11
  72.6 0.2 multiply_reduce_fusion
  72.8 2.5 %collective-permute-start.1 = (bf16[4,48,1536]{2,1,0:T(8,128)(2,1)S(1)}, bf16[4,48,1536]{2,1,0:T(8,128)(2,1)}, u32[]{:S(2)}, u32[]{:S(2)}) collective-permute-start(bf16[4,48,1536]{2,1,0:T(8,128)(2,1)S(1)} %dynamic-slice_bitcast_fusion), channel_id=1, source_target_pairs={{0,2},{1,3},{2,0},{3,1},{4,6},{5,7},{6,4},{7,5},{8,10},{9,11},{10,... | collective-permute-start | bytes 1769480 | tf_op jit(solution)/shard_map/ppermute | solution.py:163
  75.3 1.3 %fusion.5 = bf16[3,192,192]{1,2,0:T(8,128)(2,1)S(1)} fusion(bf16[3,192,128]{2,1,0:T(8,128)(2,1)S(1)} %reshape.171, bf16[3,192,128]{2,1,0:T(8,128)(2,1)S(1)} %copy-done.5, f32[3,192]{1,0:T(4,128)S(1)} %multiply_reduce_fusion, f32[3,192,192]{1,2,0:T(8,128)} %get-tuple-element.20, f32[3,192]{1,0:T(4,128)S(1)} %copy-done.8), kind=kOutput, calls=%fused_computation.10 | convolution fusion | flops 28753920 | bytes 963072 | tf_op jit(solution)/shard_map/dot_general | solution.py:15
  76.6 0.2 fusion.8
  77.0 0.3 fusion.7
  77.5 0.3 copy-done.3
  77.8 1.3 %convolution_convert_fusion.2 = bf16[3,192,128]{2,1,0:T(8,128)(2,1)S(1)} fusion(bf16[3,192,128]{2,1,0:T(8,128)(2,1)S(1)} %copy-done.3, f32[3,192]{1,0:T(4,128)S(1)} %copy-done.8, bf16[3,192,128]{2,1,0:T(8,128)(2,1)S(1)} %reshape.158, bf16[3,192,128]{2,1,0:T(8,128)(2,1)S(1)} %reshape.160, pred[192,192]{0,1:T(8,128)(4,1)} %copy-done.6), kind=kOutput, calls=%fused_computation.17 | convolution fusion | flops 57250560 | bytes 628992 | tf_op jit(solution)/shard_map/dot_general | solution.py:15
  79.2 10.0 %collective-permute-done.1 = bf16[4,48,1536]{2,1,0:T(8,128)(2,1)} collective-permute-done((bf16[4,48,1536]{2,1,0:T(8,128)(2,1)S(1)}, bf16[4,48,1536]{2,1,0:T(8,128)(2,1)}, u32[]{:S(2)}, u32[]{:S(2)}) %collective-permute-start.1) | collective-permute-done | bytes 589856 | tf_op jit(solution)/shard_map/ppermute | solution.py:163
  89.2 1.2 fusion.6
  90.4 1.8 %collective-permute-start.2 = (bf16[2,48,1536]{2,1,0:T(8,128)(2,1)S(1)}, bf16[2,48,1536]{2,1,0:T(8,128)(2,1)S(1)}, u32[]{:S(2)}, u32[]{:S(2)}) collective-permute-start(bf16[2,48,1536]{2,1,0:T(8,128)(2,1)S(1)} %dynamic-slice_bitcast_fusion.1), channel_id=1, source_target_pairs={{0,4},{1,5},{2,6},{3,7},{4,0},{5,1},{6,2},{7,3},{8,12},{9,13},{10,... | collective-permute-start | bytes 884744 | tf_op jit(solution)/shard_map/ppermute | solution.py:163
  92.2 0.1 fusion.19.x_ref
  92.3 14.6 %exchange.7 = bf16[16,112,128]{2,1,0:T(8,128)(2,1)S(1)} custom-call(bf16[16,112,128]{2,1,0:T(8,128)(2,1)S(1)} %fusion.19.x_ref), custom_call_target="tpu_custom_call" | custom-call | bytes 29360128 | tf_op jit(solution)/shard_map/exchange/pallas_call | solution.py:66
  106.9 0.9 reshape_transpose_reshape.11
  107.7 0.9 reshape_transpose_reshape.10
  108.6 0.9 reshape_transpose_reshape.9
  109.5 0.1 fusion.15
  109.6 1.4 %collective-permute-start.3 = (bf16[1,48,1536]{2,1,0:T(8,128)(2,1)S(1)}, bf16[1,48,1536]{2,1,0:T(8,128)(2,1)S(1)}, u32[]{:S(2)}, u32[]{:S(2)}) collective-permute-start(bf16[1,48,1536]{2,1,0:T(8,128)(2,1)S(1)} %constant_dynamic-slice_fusion), channel_id=1, source_target_pairs={{0,8},{1,9},{2,10},{3,11},{4,12},{5,13},{6,14},{7,15},{8,0},{9,1},... | collective-permute-start | bytes 442376 | tf_op jit(solution)/shard_map/ppermute | solution.py:163
  110.9 1.8 %convert_add_fusion.3 = f32[96,1536]{1,0:T(8,128)} fusion(bf16[96,1536]{1,0:T(8,128)(2,1)} %collective-permute-done.4, bf16[96,1536]{1,0:T(8,128)(2,1)S(1)} %convolution_convert_fusion.1), kind=kLoop, calls=%fused_computation.29 | loop fusion | flops 442368 | bytes 1179648 | tf_op jit(solution)/shard_map/add | solution.py:192
  112.8 6.8 %collective-permute-done.3 = bf16[1,48,1536]{2,1,0:T(8,128)(2,1)S(1)} collective-permute-done((bf16[1,48,1536]{2,1,0:T(8,128)(2,1)S(1)}, bf16[1,48,1536]{2,1,0:T(8,128)(2,1)S(1)}, u32[]{:S(2)}, u32[]{:S(2)}) %collective-permute-start.3) | collective-permute-done | bytes 147488 | tf_op jit(solution)/shard_map/ppermute | solution.py:163
  119.6 0.7 fusion.26
  (58 shorter events, 1.6 us)
Async XLA Ops:
  7.2 39.2 %copy-start = (bf16[96,1536]{1,0:T(8,128)(2,1)S(1)}, bf16[96,1536]{1,0:T(8,128)(2,1)}, u32[]{:S(2)}) copy-start(bf16[96,1536]{1,0:T(8,128)(2,1)} %param.10) | copy-start | bytes 884740
  7.2 52.7 %all-gather.3.cloned.1.call-start = ((), (), s32[]{:S(2)}) async-start(), calls=%async_computation | async-start | bytes 2506752 | tf_op jit(solution)/shard_map/all_gather | solution.py:113
  30.2 2.1 %copy-start.4 = (bf16[3,192,128]{2,1,0:T(8,128)(2,1)}, bf16[3,192,128]{2,1,0:T(8,128)(2,1)S(1)}, u32[]{:S(2)}) copy-start(bf16[3,192,128]{2,1,0:T(8,128)(2,1)S(1)} %reshape.162) | copy-start | bytes 442372
  30.4 1.2 copy-start.6
  31.6 0.7 copy-start.7
  46.8 2.9 %collective-permute-start = (bf16[8,48,1536]{2,1,0:T(8,128)(2,1)S(1)}, bf16[8,48,1536]{2,1,0:T(8,128)(2,1)S(1)}, u32[]{:S(2)}, u32[]{:S(2)}) collective-permute-start(bf16[8,48,1536]{2,1,0:T(8,128)(2,1)S(1)} %convolution_convert_fusion), channel_id=1, source_target_pairs={{0,1},{1,0},{2,3},{3,2},{4,5},{5,4},{6,7},{7,6},{8,9},{9,8},{10,11... | collective-permute-start | bytes 3538952 | tf_op jit(solution)/shard_map/ppermute | solution.py:152
  59.8 2.7 %copy-start.1 = (bf16[16,1,48,1536]{3,2,1,0:T(8,128)(2,1)S(1)}, bf16[16,1,48,1536]{3,2,1,0:T(8,128)(2,1)}, u32[]{:S(2)}) copy-start(bf16[16,1,48,1536]{3,2,1,0:T(8,128)(2,1)} %all-gather.3.cloned.1.call-done) | copy-start | bytes 7077892
  63.0 47.9 %collective-permute-start.4 = (bf16[96,1536]{1,0:T(8,128)(2,1)S(1)}, bf16[96,1536]{1,0:T(8,128)(2,1)}, u32[]{:S(2)}, u32[]{:S(2)}) collective-permute-start(bf16[96,1536]{1,0:T(8,128)(2,1)S(1)} %convolution_convert_fusion.1), channel_id=1, source_target_pairs={{0,16},{16,0},{1,17},{17,1},{2,18},{18,2},{3,19},{19,3},{4,20},{20... | collective-permute-start | bytes 884744 | tf_op jit(solution)/shard_map/ppermute | solution.py:191
  64.9 10.3 %copy-start.5 = (bf16[3,192,128]{2,1,0:T(8,128)(2,1)S(1)}, bf16[3,192,128]{2,1,0:T(8,128)(2,1)}, u32[]{:S(2)}) copy-start(bf16[3,192,128]{2,1,0:T(8,128)(2,1)} %copy-done.4) | copy-start | bytes 442372
  64.9 10.3 %copy-start.8 = (f32[3,192]{1,0:T(4,128)S(1)}, f32[3,192]{1,0:T(4,128)}, u32[]{:S(2)}) copy-start(f32[3,192]{1,0:T(4,128)} %copy-done.7) | copy-start | bytes 6916
  72.6 4.1 %copy-start.2 = (bf16[3,192,128]{2,1,0:T(8,128)(2,1)}, bf16[3,192,128]{2,1,0:T(8,128)(2,1)S(1)}, u32[]{:S(2)}) copy-start(bf16[3,192,128]{2,1,0:T(8,128)(2,1)S(1)} %reshape.171) | copy-start | bytes 442372
  72.8 16.4 %collective-permute-start.1 = (bf16[4,48,1536]{2,1,0:T(8,128)(2,1)S(1)}, bf16[4,48,1536]{2,1,0:T(8,128)(2,1)}, u32[]{:S(2)}, u32[]{:S(2)}) collective-permute-start(bf16[4,48,1536]{2,1,0:T(8,128)(2,1)S(1)} %dynamic-slice_bitcast_fusion), channel_id=1, source_target_pairs={{0,2},{1,3},{2,0},{3,1},{4,6},{5,7},{6,4},{7,5},{8,10},{9,11},{10,... | collective-permute-start | bytes 1769480 | tf_op jit(solution)/shard_map/ppermute | solution.py:163
  76.8 0.9 copy-start.3
  90.4 19.0 %collective-permute-start.2 = (bf16[2,48,1536]{2,1,0:T(8,128)(2,1)S(1)}, bf16[2,48,1536]{2,1,0:T(8,128)(2,1)S(1)}, u32[]{:S(2)}, u32[]{:S(2)}) collective-permute-start(bf16[2,48,1536]{2,1,0:T(8,128)(2,1)S(1)} %dynamic-slice_bitcast_fusion.1), channel_id=1, source_target_pairs={{0,4},{1,5},{2,6},{3,7},{4,0},{5,1},{6,2},{7,3},{8,12},{9,13},{10,... | collective-permute-start | bytes 884744 | tf_op jit(solution)/shard_map/ppermute | solution.py:163
  109.6 10.0 %collective-permute-start.3 = (bf16[1,48,1536]{2,1,0:T(8,128)(2,1)S(1)}, bf16[1,48,1536]{2,1,0:T(8,128)(2,1)S(1)}, u32[]{:S(2)}, u32[]{:S(2)}) collective-permute-start(bf16[1,48,1536]{2,1,0:T(8,128)(2,1)S(1)} %constant_dynamic-slice_fusion), channel_id=1, source_target_pairs={{0,8},{1,9},{2,10},{3,11},{4,12},{5,13},{6,14},{7,15},{8,0},{9,1},... | collective-permute-start | bytes 442376 | tf_op jit(solution)/shard_map/ppermute | solution.py:163
Sparse Core Ops, SparseCore 0:
  10.3 49.4 all-gather.2

commit v5 on v4

--- a/solution.py
+++ b/solution.py
@@ -147,29 +147,34 @@
         picked = lax.dynamic_index_in_dim(pairs, side, 1, keepdims=False)
         return dot(picked, out_weight, (((2,), (0,)), ((), ())))
 
-    sent = terms(1 - place % 2).astype(LOW)
-    _, grad_all = lax.optimization_barrier((sent, grad_all))
-    total = terms(place % 2) + lax.ppermute(
-        sent, "seq", [(i, i ^ 1) for i in range(n)]
-    ).astype(jnp.float32)
-    mixed_grad = dot(grad_all, out_weight, (((1,), (1,)), ((), ()))).astype(LOW)
-    total, mixed_grad = lax.optimization_barrier((total, mixed_grad))
-    step = 2
-    while step < n:
+    def pass_on(sent, step):
+        moved = lax.ppermute(sent, "seq", [(i, i ^ step) for i in range(n)])
+        return moved.astype(jnp.float32)
+
+    def split(total, step):
         halves = total.astype(LOW).reshape(n // step // 2, 2, own * span, total.shape[2])
         side = (place // step) % 2
         sent = lax.dynamic_index_in_dim(halves, 1 - side, 1, keepdims=False)
-        kept = lax.dynamic_index_in_dim(halves, side, 1, keepdims=False)
-        total = kept.astype(jnp.float32) + lax.ppermute(
-            sent, "seq", [(i, i ^ step) for i in range(n)]
-        ).astype(jnp.float32)
-        step = 2 * step
-    mixed_out = total.astype(LOW)
+        return sent, lax.dynamic_index_in_dim(halves, side, 1, keepdims=False)
+
+    def halve(total, step):
+        if step >= n:
+            return total
+        sent, kept = split(total, step)
+        return kept.astype(jnp.float32) + pass_on(sent, step)
+
+    sent = terms(1 - place % 2).astype(LOW)
+    _, grad_all = lax.optimization_barrier((sent, grad_all))
+    total = terms(place % 2) + pass_on(sent, 1)
+    mixed_grad = dot(grad_all, out_weight, (((1,), (1,)), ((), ()))).astype(LOW)
+    total, mixed_grad = lax.optimization_barrier((total, mixed_grad))
 
     mixed_grad = (
         mixed_grad.reshape(frames, n, per, part).swapaxes(0, 1).reshape(n, frames * per, part)
     )
-    grad = to_places(exchange(mixed_grad, 2).swapaxes(0, 1).reshape(frames, per, width))
+    grad = exchange(mixed_grad, 2)
+    total, grad = lax.optimization_barrier((halve(total, 2), grad))
+    grad = to_places(grad.swapaxes(0, 1).reshape(frames, per, width))
 
     value_grad = dot(probs_low, grad, across).astype(LOW)
     through = dot(grad, value, inside)
@@ -179,9 +184,15 @@
     score_grad = (probs * (through - inner)).astype(LOW)
     query_grad = (dot(score_grad, key, onward) * factor).astype(LOW)
     key_grad = (dot(score_grad, query, across) * factor).astype(LOW)
-    home = exchange(
-        jnp.concatenate([to_frames(x) for x in (query_grad, key_grad, value_grad)], axis=1), 3
-    )
+    home = jnp.concatenate([to_frames(x) for x in (query_grad, key_grad, value_grad)], axis=1)
+    total, home = lax.optimization_barrier((halve(total, 4), home))
+    home = exchange(home, 3)
+    step = 8
+    while step < n:
+        total = halve(total, step)
+        step = 2 * step
+    total, home = lax.optimization_barrier((total, home))
+    mixed_out = total.astype(LOW)
     q_back, k_back, v_back = (
         from_blocks(home[:, i * rows : (i + 1) * rows]) for i in range(3)
     )

time: 128 us -> 122 us (0.953)
  waiting for transfers between devices: 28.6 us -> 17 us
  Pallas kernels: 51.7 us -> 59.4 us
  starting transfers between devices: 7.24 us -> 4.9 us
    ppermute x4, waiting for transfers between devices: 19.2 us -> 9.35 us  [pass_on(): moved = lax.ppermute(sent, 'seq', [(i, i ^ step) for i in range(n)])]
    pallas_call x4, Pallas kernels: 51.7 us -> 59.4 us  [exchange(): pl.pallas_call(functools.partial(exchange_kernel, n), out_shape=jax.Shape...]
    ppermute x4, starting transfers between devices: 5.67 us -> 3.33 us  [pass_on(): moved = lax.ppermute(sent, 'seq', [(i, i ^ step) for i in range(n)])]
    add x0 -> x3, other arithmetic: none -> 1.98 us  [halve(): return kept.astype(jnp.float32) + pass_on(sent, step)]
    all_gather x1, waiting for transfers between devices: 8.75 us -> 7 us  [local(): grad_all = lax.all_gather(out_grad[0], 'seq', axis=0, tiled=True)]
  transfers between devices with their start and end apart: 6 -> 6, of which waited for: 4 -> 3; matrix products, arithmetic and copies ran while one was open for 16% -> 14% of each run, Pallas kernels for 41% -> 49%
where the time goes in v5:
time: 122 us; the launch traced here: 121 us
  Pallas kernels  59.4 us (49%)
  waiting for transfers between devices  17 us (14%)
  between operations  14.8 us (12%)
  local copies, waits for them, and re-layouts  11.6 us (10%)
  matrix products  10.1 us (8%)
  starting transfers between devices  4.9 us (4%)
  other arithmetic  3.35 us (3%)
    pallas_call x4, Pallas kernels, exchange(): pl.pallas_call(functools.partial(exchange_kernel, n), out_shape=jax.Shape...  59.4 us
    ppermute x4, waiting for transfers between devices, pass_on(): moved = lax.ppermute(sent, 'seq', [(i, i ^ step) for i in range(n)])  9.35 us
    dot_general x9, matrix products, dot(): return lax.dot_general(a, b, dims, preferred_element_type=jnp.float32)  8.88 us
    all_gather x1, waiting for transfers between devices, local(): grad_all = lax.all_gather(out_grad[0], 'seq', axis=0, tiled=True)  7 us
    another operation x3, local copies, waits for them, and re-layouts, to_blocks(): x[0].reshape(own, n, per * heads, HEAD).swapaxes(0, 1)  3.34 us
    ppermute x4, starting transfers between devices, pass_on(): moved = lax.ppermute(sent, 'seq', [(i, i ^ step) for i in range(n)])  3.33 us
    another operation x3, local copies, waits for them, and re-layouts, from_blocks(): x.reshape(n, own, per, width).swapaxes(0, 1).reshape(1, own, span, width)  2.55 us
  transfers between devices with their start and end apart: 6, of which 3 were waited for; matrix products, arithmetic and copies ran while one was open for 14% of the time, Pallas kernels for 49%

profile of v5, /device:TPU:0, one launch (start us, length us, event | category | flops | bytes accessed | tf_op | source)
XLA Modules:
  0.0 121.2 jit_solution(3784905158503206970)
XLA Ops:
  7.2 0.7 all-gather.3.cloned.1.call-update
  7.9 0.7 broadcast_in_dim.19
  8.7 0.1 eq.44
  8.8 0.1 eq.48
  8.8 1.1 reshape_transpose_reshape_squeeze.9
  10.0 1.1 reshape_transpose_reshape_squeeze.10
  11.1 1.1 reshape_transpose_reshape_squeeze.11
  12.2 0.1 fusion.12.x_ref
  12.3 17.5 %exchange.4 = bf16[16,112,128]{2,1,0:T(8,128)(2,1)S(1)} custom-call(bf16[16,112,128]{2,1,0:T(8,128)(2,1)S(1)} %fusion.12.x_ref), custom_call_target="tpu_custom_call" | custom-call | bytes 29360128 | tf_op jit(solution)/shard_map/exchange/pallas_call | solution.py:66
  30.3 0.1 compare_and_fusion
  30.5 1.2 fusion.30
  31.7 0.6 copy-done.13
  32.2 0.6 convolution_convert_fusion.4
  32.9 0.6 copy-done.4
  33.5 0.2 reshape_reshape.9
  33.8 13.9 %exchange.5 = bf16[16,48,128]{2,1,0:T(8,128)(2,1)S(1)} custom-call(bf16[16,48,128]{2,1,0:T(8,128)(2,1)S(1)} %pad.15.x_ref), custom_call_target="tpu_custom_call" | custom-call | bytes 12582912 | tf_op jit(solution)/shard_map/exchange/pallas_call | solution.py:66
  47.8 0.4 constant_dynamic-slice_fusion.2
  48.3 0.4 convolution_convert_fusion
  48.8 2.8 %collective-permute-done = bf16[8,48,1536]{2,1,0:T(8,128)(2,1)S(1)} collective-permute-done((bf16[8,48,1536]{2,1,0:T(8,128)(2,1)S(1)}, bf16[8,48,1536]{2,1,0:T(8,128)(2,1)S(1)}, u32[]{:S(2)}, u32[]{:S(2)}) %collective-permute-start) | collective-permute-done | bytes 1179680 | tf_op jit(solution)/shard_map/ppermute | solution.py:151
  51.6 1.5 %convert_add_fusion = bf16[8,48,1536]{2,1,0:T(8,128)(2,1)} fusion(bf16[8,48,1536]{2,1,0:T(8,128)(2,1)S(1)} %collective-permute-done, bf16[96,1536]{1,0:T(8,128)(2,1)S(1)} %copy-done, bf16[8,1,48,96]{3,1,0,2:T(2,128)(2,1)S(1)} %get-tuple-element.29), kind=kOutput, calls=%fused_computation.2 | convolution fusion | flops 115015680 | bytes 2727936 | tf_op jit(solution)/shard_map/dot_general | solution.py:15
  53.1 7.0 %all-gather.3.cloned.1.call-done = bf16[16,1,48,1536]{3,2,1,0:T(8,128)(2,1)} async-done(((bf16[1,1,48,1536]{3,2,1,0:T(8,128)(2,1)}), bf16[16,1,48,1536]{3,2,1,0:T(8,128)(2,1)}) %all-gather.3.cloned.1.call-update) | async-done | bytes 2359312 | tf_op jit(solution)/shard_map/all_gather | solution.py:113
  60.1 2.7 %convolution_convert_fusion.3 = bf16[768,96]{0,1:T(8,128)(2,1)S(1)} fusion(bf16[768,1536]{1,0:T(8,128)(2,1)} %bitcast.89, bf16[96,1536]{1,0:T(8,128)(2,1)S(1)} %copy-done), kind=kOutput, calls=%fused_computation.17 | convolution fusion | flops 226566144 | bytes 2801664 | tf_op jit(solution)/shard_map/dot_general | solution.py:15
  62.8 0.9 dynamic-slice_bitcast_fusion
  63.6 1.1 collective-permute-start.1
  64.7 0.1 copy.76
  64.9 0.2 reshape.178
  65.1 0.5 convolution_convert_fusion.1
  65.6 1.5 %collective-permute-start.4 = (bf16[96,1536]{1,0:T(8,128)(2,1)S(1)}, bf16[96,1536]{1,0:T(8,128)(2,1)S(1)}, u32[]{:S(2)}, u32[]{:S(2)}) collective-permute-start(bf16[96,1536]{1,0:T(8,128)(2,1)S(1)} %convolution_convert_fusion.1), channel_id=1, source_target_pairs={{0,16},{16,0},{1,17},{17,1},{2,18},{18,2},{3,19},{19,3},{4,20},{20... | collective-permute-start | bytes 884744 | tf_op jit(solution)/shard_map/ppermute | solution.py:202
  67.1 0.2 copy.63
  67.3 0.1 reshape.167
  67.6 14.0 %exchange.6 = bf16[16,48,128]{2,1,0:T(8,128)(2,1)S(1)} custom-call(bf16[16,48,128]{2,1,0:T(8,128)(2,1)S(1)} %pad.16.x_ref), custom_call_target="tpu_custom_call" | custom-call | bytes 12582912 | tf_op jit(solution)/shard_map/exchange/pallas_call | solution.py:66
  81.6 1.2 convert_add_fusion.1
  82.9 0.2 reshape_reshape.11
  83.2 0.2 multiply_reduce_fusion
  83.4 1.3 %fusion.5 = bf16[3,192,192]{1,2,0:T(8,128)(2,1)S(1)} fusion(bf16[3,192,128]{2,1,0:T(8,128)(2,1)S(1)} %reshape.170, bf16[3,192,128]{2,1,0:T(8,128)(2,1)S(1)} %copy-done.11, f32[3,192]{1,0:T(4,128)S(1)} %multiply_reduce_fusion, f32[3,192,192]{1,2,0:T(8,128)} %get-tuple-element.32, f32[3,192]{1,0:T(4,128)S(1)} %copy-done.14), kind=kOutput, calls=%fused_computation.10 | convolution fusion | flops 28753920 | bytes 963072 | tf_op jit(solution)/shard_map/dot_general | solution.py:15
  84.7 0.3 fusion.6
  85.1 0.2 fusion.7
  85.6 1.0 collective-permute-start.2
  86.6 1.3 %convolution_convert_fusion.2 = bf16[3,192,128]{2,1,0:T(8,128)(2,1)S(1)} fusion(bf16[3,192,128]{2,1,0:T(8,128)(2,1)S(1)} %reshape.170, f32[3,192]{1,0:T(4,128)S(1)} %copy-done.14, bf16[3,192,128]{2,1,0:T(8,128)(2,1)S(1)} %copy-done.9, bf16[3,192,128]{2,1,0:T(8,128)(2,1)S(1)} %copy-done.7, pred[192,192]{0,1:T(8,128)(4,1)} %copy-done.12), kind=kOutput, calls=%fused_computation.16 | convolution fusion | flops 57250560 | bytes 628992 | tf_op jit(solution)/shard_map/dot_general | solution.py:15
  88.1 0.1 pad_maximum_fusion
  88.2 6.6 %collective-permute-done.2 = bf16[2,48,1536]{2,1,0:T(8,128)(2,1)S(1)} collective-permute-done((bf16[2,48,1536]{2,1,0:T(8,128)(2,1)S(1)}, bf16[2,48,1536]{2,1,0:T(8,128)(2,1)S(1)}, u32[]{:S(2)}, u32[]{:S(2)}) %collective-permute-start.2) | collective-permute-done | bytes 294944 | tf_op jit(solution)/shard_map/ppermute | solution.py:151
  94.8 1.2 collective-permute-start.3
  96.0 0.9 convert_add_fusion.3
  96.9 14.1 %exchange.7 = bf16[16,112,128]{2,1,0:T(8,128)(2,1)S(1)} custom-call(bf16[16,112,128]{2,1,0:T(8,128)(2,1)S(1)} %pad.17.x_ref), custom_call_target="tpu_custom_call" | custom-call | bytes 29360128 | tf_op jit(solution)/shard_map/exchange/pallas_call | solution.py:66
  111.0 0.7 convert_add_fusion.4
  111.8 0.9 reshape_transpose_reshape.11
  112.6 0.9 reshape_transpose_reshape.10
  113.5 0.9 reshape_transpose_reshape.9
  (70 shorter events, 1.6 us)
Async XLA Ops:
  7.2 41.1 %copy-start = (bf16[96,1536]{1,0:T(8,128)(2,1)S(1)}, bf16[96,1536]{1,0:T(8,128)(2,1)}, u32[]{:S(2)}) copy-start(bf16[96,1536]{1,0:T(8,128)(2,1)} %param.10) | copy-start | bytes 884740
  7.2 52.9 %all-gather.3.cloned.1.call-start = ((), (), s32[]{:S(2)}) async-start(), calls=%async_computation | async-start | bytes 2506752 | tf_op jit(solution)/shard_map/all_gather | solution.py:113
  30.0 2.8 %copy-start.6 = (bf16[3,192,128]{2,1,0:T(8,128)(2,1)}, bf16[3,192,128]{2,1,0:T(8,128)(2,1)S(1)}, u32[]{:S(2)}) copy-start(bf16[3,192,128]{2,1,0:T(8,128)(2,1)S(1)} %reshape.160) | copy-start | bytes 442372
  30.2 1.5 %copy-start.10 = (bf16[3,192,128]{2,1,0:T(8,128)(2,1)}, bf16[3,192,128]{2,1,0:T(8,128)(2,1)S(1)}, u32[]{:S(2)}) copy-start(bf16[3,192,128]{2,1,0:T(8,128)(2,1)S(1)} %reshape.162) | copy-start | bytes 442372
  30.3 1.3 %copy-start.8 = (bf16[3,192,128]{2,1,0:T(8,128)(2,1)}, bf16[3,192,128]{2,1,0:T(8,128)(2,1)S(1)}, u32[]{:S(2)}) copy-start(bf16[3,192,128]{2,1,0:T(8,128)(2,1)S(1)} %reshape.158) | copy-start | bytes 442372
  30.4 2.5 %copy-start.12 = (pred[192,192]{0,1:T(8,128)(4,1)}, pred[192,192]{0,1:T(8,128)(4,1)S(1)}, u32[]{:S(2)}) copy-start(pred[192,192]{0,1:T(8,128)(4,1)S(1)} %compare_and_fusion) | copy-start | bytes 110596
  31.6 0.6 copy-start.13
  32.9 0.7 copy-start.4
  48.7 2.9 %collective-permute-start = (bf16[8,48,1536]{2,1,0:T(8,128)(2,1)S(1)}, bf16[8,48,1536]{2,1,0:T(8,128)(2,1)S(1)}, u32[]{:S(2)}, u32[]{:S(2)}) collective-permute-start(bf16[8,48,1536]{2,1,0:T(8,128)(2,1)S(1)} %convolution_convert_fusion), channel_id=1, source_target_pairs={{0,1},{1,0},{2,3},{3,2},{4,5},{5,4},{6,7},{7,6},{8,9},{9,8},{10,11... | collective-permute-start | bytes 3538952 | tf_op jit(solution)/shard_map/ppermute | solution.py:151
  60.1 2.7 %copy-start.2 = (bf16[8,48,1536]{2,1,0:T(8,128)(2,1)S(1)}, bf16[8,48,1536]{2,1,0:T(8,128)(2,1)}, u32[]{:S(2)}) copy-start(bf16[8,48,1536]{2,1,0:T(8,128)(2,1)} %convert_add_fusion) | copy-start | bytes 3538948
  60.1 4.9 %copy-start.1 = (bf16[16,1,48,1536]{3,2,1,0:T(8,128)(2,1)S(1)}, bf16[16,1,48,1536]{3,2,1,0:T(8,128)(2,1)}, u32[]{:S(2)}) copy-start(bf16[16,1,48,1536]{3,2,1,0:T(8,128)(2,1)} %all-gather.3.cloned.1.call-done) | copy-start | bytes 7077892
  63.6 18.0 %collective-permute-start.1 = (bf16[4,48,1536]{2,1,0:T(8,128)(2,1)}, bf16[4,48,1536]{2,1,0:T(8,128)(2,1)}, u32[]{:S(2)}, u32[]{:S(2)}) collective-permute-start(bf16[4,48,1536]{2,1,0:T(8,128)(2,1)} %dynamic-slice_bitcast_fusion), channel_id=1, source_target_pairs={{0,2},{1,3},{2,0},{3,1},{4,6},{5,7},{6,4},{7,5},{8,10},{9,11},{10,... | collective-permute-start | bytes 1769480 | tf_op jit(solution)/shard_map/ppermute | solution.py:151
  65.6 16.0 %copy-start.3 = (bf16[8,48,1536]{2,1,0:T(8,128)(2,1)S(1)}, bf16[8,48,1536]{2,1,0:T(8,128)(2,1)}, u32[]{:S(2)}) copy-start(bf16[8,48,1536]{2,1,0:T(8,128)(2,1)} %convert_add_fusion) | copy-start | bytes 3538948
  65.6 30.4 %collective-permute-start.4 = (bf16[96,1536]{1,0:T(8,128)(2,1)S(1)}, bf16[96,1536]{1,0:T(8,128)(2,1)S(1)}, u32[]{:S(2)}, u32[]{:S(2)}) collective-permute-start(bf16[96,1536]{1,0:T(8,128)(2,1)S(1)} %convolution_convert_fusion.1), channel_id=1, source_target_pairs={{0,16},{16,0},{1,17},{17,1},{2,18},{18,2},{3,19},{19,3},{4,20},{20... | collective-permute-start | bytes 884744 | tf_op jit(solution)/shard_map/ppermute | solution.py:202
  67.5 15.7 %copy-start.5 = (bf16[3,192,128]{2,1,0:T(8,128)(2,1)S(1)}, bf16[3,192,128]{2,1,0:T(8,128)(2,1)}, u32[]{:S(2)}) copy-start(bf16[3,192,128]{2,1,0:T(8,128)(2,1)} %copy-done.4) | copy-start | bytes 442372
  67.5 15.9 %copy-start.11 = (bf16[3,192,128]{2,1,0:T(8,128)(2,1)S(1)}, bf16[3,192,128]{2,1,0:T(8,128)(2,1)}, u32[]{:S(2)}) copy-start(bf16[3,192,128]{2,1,0:T(8,128)(2,1)} %copy-done.10) | copy-start | bytes 442372
  67.5 15.9 %copy-start.14 = (f32[3,192]{1,0:T(4,128)S(1)}, f32[3,192]{1,0:T(4,128)}, u32[]{:S(2)}) copy-start(f32[3,192]{1,0:T(4,128)} %copy-done.13) | copy-start | bytes 6916
  82.9 1.9 %copy-start.7 = (bf16[3,192,128]{2,1,0:T(8,128)(2,1)S(1)}, bf16[3,192,128]{2,1,0:T(8,128)(2,1)}, u32[]{:S(2)}) copy-start(bf16[3,192,128]{2,1,0:T(8,128)(2,1)} %copy-done.6) | copy-start | bytes 442372
  82.9 2.1 %copy-start.9 = (bf16[3,192,128]{2,1,0:T(8,128)(2,1)S(1)}, bf16[3,192,128]{2,1,0:T(8,128)(2,1)}, u32[]{:S(2)}) copy-start(bf16[3,192,128]{2,1,0:T(8,128)(2,1)} %copy-done.8) | copy-start | bytes 442372
  85.6 9.1 %collective-permute-start.2 = (bf16[2,48,1536]{2,1,0:T(8,128)(2,1)S(1)}, bf16[2,48,1536]{2,1,0:T(8,128)(2,1)S(1)}, u32[]{:S(2)}, u32[]{:S(2)}) collective-permute-start(bf16[2,48,1536]{2,1,0:T(8,128)(2,1)S(1)} %dynamic-slice_bitcast_fusion.1), channel_id=1, source_target_pairs={{0,4},{1,5},{2,6},{3,7},{4,0},{5,1},{6,2},{7,3},{8,12},{9,13},{10,... | collective-permute-start | bytes 884744 | tf_op jit(solution)/shard_map/ppermute | solution.py:151
  94.8 16.2 %collective-permute-start.3 = (bf16[1,48,1536]{2,1,0:T(8,128)(2,1)S(1)}, bf16[1,48,1536]{2,1,0:T(8,128)(2,1)S(1)}, u32[]{:S(2)}, u32[]{:S(2)}) collective-permute-start(bf16[1,48,1536]{2,1,0:T(8,128)(2,1)S(1)} %constant_dynamic-slice_fusion), channel_id=1, source_target_pairs={{0,8},{1,9},{2,10},{3,11},{4,12},{5,13},{6,14},{7,15},{8,0},{9,1},... | collective-permute-start | bytes 442376 | tf_op jit(solution)/shard_map/ppermute | solution.py:151
Sparse Core Ops, SparseCore 0:
  10.3 49.7 all-gather.2

commit v6 on v5

--- a/solution.py
+++ b/solution.py
@@ -84,6 +84,44 @@
     return moved[:, :rows, :lanes]
 
 
+def swap_kernel(step, x_ref, o_ref, send_sem, recv_sem):
+    me = lax.axis_index("seq")
+    partner = me + step - 2 * step * lax.rem(lax.div(me, step), 2)
+    target = (lax.axis_index("dp"), partner)
+    barrier = pltpu.get_barrier_semaphore()
+    pl.semaphore_signal(
+        barrier, inc=1, device_id=target, device_id_type=pl.DeviceIdType.MESH
+    )
+    pl.semaphore_wait(barrier, 1)
+    copy = pltpu.make_async_remote_copy(
+        src_ref=x_ref,
+        dst_ref=o_ref,
+        send_sem=send_sem,
+        recv_sem=recv_sem,
+        device_id=target,
+        device_id_type=pl.DeviceIdType.MESH,
+    )
+    copy.start()
+    copy.wait()
+
+
+def swap(block, step, which):
+    return pl.pallas_call(
+        functools.partial(swap_kernel, step),
+        out_shape=jax.ShapeDtypeStruct(block.shape, block.dtype),
+        in_specs=[pl.BlockSpec(memory_space=pltpu.VMEM)],
+        out_specs=pl.BlockSpec(memory_space=pltpu.VMEM),
+        scratch_shapes=[pltpu.SemaphoreType.DMA, pltpu.SemaphoreType.DMA],
+        compiler_params=pltpu.CompilerParams(
+            collective_id=which, has_side_effects=True, vmem_limit_bytes=40 * 1024 * 1024
+        ),
+        cost_estimate=pl.CostEstimate(
+            flops=0, bytes_accessed=4 * block.size, transcendentals=0
+        ),
+        name="swap",
+    )(block)
+
+
 def local(queries, key_field, value_field, out_grad, out_weight, frame_video):
     n = lax.axis_size("seq")
     _, own, span, width = queries.shape
@@ -164,8 +202,10 @@
         return kept.astype(jnp.float32) + pass_on(sent, step)
 
     sent = terms(1 - place % 2).astype(LOW)
-    _, grad_all = lax.optimization_barrier((sent, grad_all))
     total = terms(place % 2) + pass_on(sent, 1)
+    sent, kept = split(total, 2)
+    total = kept.astype(jnp.float32) + swap(sent, 2, 4).astype(jnp.float32)
+    _, grad_all = lax.optimization_barrier((total, grad_all))
     mixed_grad = dot(grad_all, out_weight, (((1,), (1,)), ((), ()))).astype(LOW)
     total, mixed_grad = lax.optimization_barrier((total, mixed_grad))
 
@@ -173,7 +213,7 @@
         mixed_grad.reshape(frames, n, per, part).swapaxes(0, 1).reshape(n, frames * per, part)
     )
     grad = exchange(mixed_grad, 2)
-    total, grad = lax.optimization_barrier((halve(total, 2), grad))
+    total, grad = lax.optimization_barrier((halve(total, 4), grad))
     grad = to_places(grad.swapaxes(0, 1).reshape(frames, per, width))
 
     value_grad = dot(probs_low, grad, across).astype(LOW)
@@ -185,7 +225,6 @@
     query_grad = (dot(score_grad, key, onward) * factor).astype(LOW)
     key_grad = (dot(score_grad, query, across) * factor).astype(LOW)
     home = jnp.concatenate([to_frames(x) for x in (query_grad, key_grad, value_grad)], axis=1)
-    total, home = lax.optimization_barrier((halve(total, 4), home))
     home = exchange(home, 3)
     step = 8
     while step < n:

time: 122 us -> 119 us (0.975)
  waiting for transfers between devices: 17 us -> 5.09 us
  Pallas kernels: 59.4 us -> 67.6 us
    pallas_call x0 -> x1, Pallas kernels: none -> 15.4 us  [swap(): pl.pallas_call(functools.partial(swap_kernel, step), out_shape=jax.ShapeD...]
    ppermute x4 -> x3, waiting for transfers between devices: 9.35 us -> 1.78 us  [pass_on(): moved = lax.ppermute(sent, 'seq', [(i, i ^ step) for i in range(n)])]
    pallas_call x4, Pallas kernels: 59.4 us -> 52.1 us  [exchange(): pl.pallas_call(functools.partial(exchange_kernel, n), out_shape=jax.Shape...]
    all_gather x1, waiting for transfers between devices: 7 us -> 0.02 us  [local(): grad_all = lax.all_gather(out_grad[0], 'seq', axis=0, tiled=True)]
    ppermute x1, waiting for transfers between devices: 0.01 us -> 2.6 us  [local(): other = lax.ppermute(share, 'dp', [(0, 1), (1, 0)])]
    ppermute x4 -> x3, starting transfers between devices: 3.33 us -> 3.51 us  [pass_on(): moved = lax.ppermute(sent, 'seq', [(i, i ^ step) for i in range(n)])]
  transfers between devices with their start and end apart: 6 -> 5, of which waited for: 3 -> 2; matrix products, arithmetic and copies ran while one was open for 14% -> 16% of each run, Pallas kernels for 49% -> 57%
where the time goes in v6:
time: 119 us; the launch traced here: 118 us
  Pallas kernels  67.6 us (57%)
  between operations  14.8 us (12%)
  local copies, waits for them, and re-layouts  12.5 us (11%)
  matrix products  9.82 us (8%)
  waiting for transfers between devices  5.09 us (4%)
  starting transfers between devices  4.69 us (4%)
  other arithmetic  3.26 us (3%)
    pallas_call x4, Pallas kernels, exchange(): pl.pallas_call(functools.partial(exchange_kernel, n), out_shape=jax.Shape...  52.1 us
    pallas_call x1, Pallas kernels, swap(): pl.pallas_call(functools.partial(swap_kernel, step), out_shape=jax.ShapeD...  15.4 us
    dot_general x9, matrix products, dot(): return lax.dot_general(a, b, dims, preferred_element_type=jnp.float32)  8.63 us
    ppermute x3, starting transfers between devices, pass_on(): moved = lax.ppermute(sent, 'seq', [(i, i ^ step) for i in range(n)])  3.51 us
    another operation x3, local copies, waits for them, and re-layouts, to_blocks(): x[0].reshape(own, n, per * heads, HEAD).swapaxes(0, 1)  3.34 us
    ppermute x1, waiting for transfers between devices, local(): other = lax.ppermute(share, 'dp', [(0, 1), (1, 0)])  2.6 us
    another operation x3, local copies, waits for them, and re-layouts, from_blocks(): x.reshape(n, own, per, width).swapaxes(0, 1).reshape(1, own, span, width)  2.55 us
  transfers between devices with their start and end apart: 5, of which 2 were waited for; matrix products, arithmetic and copies ran while one was open for 16% of the time, Pallas kernels for 57%

profile of v6, /device:TPU:0, one launch (start us, length us, event | category | flops | bytes accessed | tf_op | source)
XLA Modules:
  0.0 117.7 jit_solution(16192797674243082773)
XLA Ops:
  7.2 0.7 all-gather.3.cloned.1.call-update
  7.9 1.1 reshape_transpose_reshape_squeeze.11
  9.0 1.1 reshape_transpose_reshape_squeeze.10
  10.2 1.1 reshape_transpose_reshape_squeeze.9
  11.3 0.1 fusion.15.x_ref
  11.4 16.3 %exchange.4 = bf16[16,112,128]{2,1,0:T(8,128)(2,1)S(1)} custom-call(bf16[16,112,128]{2,1,0:T(8,128)(2,1)S(1)} %fusion.15.x_ref), custom_call_target="tpu_custom_call" | custom-call | bytes 29360128 | tf_op jit(solution)/shard_map/exchange/pallas_call | solution.py:66
  28.2 0.1 eq.48
  28.3 0.1 broadcast_in_dim.19
  28.4 0.1 eq.44
  28.4 0.1 compare_and_fusion
  28.6 1.2 %fusion.35 = (f32[3,192]{1,0:T(4,128)S(1)}, f32[3,192,192]{1,2,0:T(8,128)}) fusion(bf16[3,192,128]{2,1,0:T(8,128)(2,1)S(1)} %reshape.158, bf16[3,192,128]{2,1,0:T(8,128)(2,1)S(1)} %reshape.160, pred[192,192]{0,1:T(8,128)(4,1)S(1)} %compare_and_fusion), kind=kOutput, calls=%fused_computation.56 | convolution fusion | flops 28754112 | bytes 776448 | tf_op jit(solution)/shard_map/sub | solution.py:168
  29.8 0.6 convolution_convert_fusion.4
  30.5 0.6 copy-done.2
  31.1 0.2 reshape_reshape.9
  31.4 14.0 %exchange.5 = bf16[16,48,128]{2,1,0:T(8,128)(2,1)S(1)} custom-call(bf16[16,48,128]{2,1,0:T(8,128)(2,1)S(1)} %pad.15.x_ref), custom_call_target="tpu_custom_call" | custom-call | bytes 12582912 | tf_op jit(solution)/shard_map/exchange/pallas_call | solution.py:66
  45.6 0.4 constant_dynamic-slice_fusion.2
  46.0 0.4 convolution_convert_fusion
  46.5 0.1 collective-permute-start
  46.6 0.1 copy.79
  46.8 0.8 reshape.178
  47.6 1.8 %collective-permute-done = bf16[8,48,1536]{2,1,0:T(8,128)(2,1)S(1)} collective-permute-done((bf16[8,48,1536]{2,1,0:T(8,128)(2,1)S(1)}, bf16[8,48,1536]{2,1,0:T(8,128)(2,1)S(1)}, u32[]{:S(2)}, u32[]{:S(2)}) %collective-permute-start) | collective-permute-done | bytes 1179680 | tf_op jit(solution)/shard_map/ppermute | solution.py:189
  49.4 0.4 add_convert_fusion
  49.9 15.4 %swap.1 = bf16[4,48,1536]{2,1,0:T(8,128)(2,1)S(1)} custom-call(bf16[4,48,1536]{2,1,0:T(8,128)(2,1)S(1)} %dynamic-slice_bitcast_fusion.x_ref), custom_call_target="tpu_custom_call" | custom-call | bytes 1179648 | tf_op jit(solution)/shard_map/swap/pallas_call | solution.py:109
  65.3 0.2 convert_add_fusion
  65.5 2.5 %convolution_convert_fusion.3 = bf16[768,96]{0,1:T(8,128)(2,1)S(1)} fusion(bf16[768,1536]{1,0:T(8,128)(2,1)} %bitcast.91, bf16[96,1536]{1,0:T(8,128)(2,1)S(1)} %copy-done), kind=kOutput, calls=%fused_computation.17 | convolution fusion | flops 226566144 | bytes 2801664 | tf_op jit(solution)/shard_map/dot_general | solution.py:15
  68.0 0.7 dynamic-slice_bitcast_fusion.1
  68.7 1.6 %collective-permute-start.1 = (bf16[2,48,1536]{2,1,0:T(8,128)(2,1)}, bf16[2,48,1536]{2,1,0:T(8,128)(2,1)}, u32[]{:S(2)}, u32[]{:S(2)}) collective-permute-start(bf16[2,48,1536]{2,1,0:T(8,128)(2,1)} %dynamic-slice_bitcast_fusion.1), channel_id=1, source_target_pairs={{0,4},{1,5},{2,6},{3,7},{4,0},{5,1},{6,2},{7,3},{8,12},{9,13},{10,... | collective-permute-start | bytes 884744 | tf_op jit(solution)/shard_map/ppermute | solution.py:189
  70.4 0.8 copy.66
  71.2 1.1 reshape.168
  72.4 10.0 %exchange.6 = bf16[16,48,128]{2,1,0:T(8,128)(2,1)S(1)} custom-call(bf16[16,48,128]{2,1,0:T(8,128)(2,1)S(1)} %pad.16.x_ref), custom_call_target="tpu_custom_call" | custom-call | bytes 12582912 | tf_op jit(solution)/shard_map/exchange/pallas_call | solution.py:66
  82.4 1.5 %convolution_convert_fusion.1 = bf16[96,1536]{1,0:T(8,128)(2,1)S(1)} fusion(bf16[768,96]{1,0:T(8,128)(2,1)} %reshape.178, bf16[768,1536]{1,0:T(8,128)(2,1)S(1)} %bitcast.92), kind=kOutput, calls=%fused_computation.3 | convolution fusion | flops 226639872 | bytes 2801664 | tf_op jit(solution)/shard_map/dot_general | solution.py:15
  83.9 1.1 collective-permute-start.3
  85.1 1.0 convert_add_fusion.1
  86.1 1.8 %collective-permute-start.2 = (bf16[1,48,1536]{2,1,0:T(8,128)(2,1)S(1)}, bf16[1,48,1536]{2,1,0:T(8,128)(2,1)S(1)}, u32[]{:S(2)}, u32[]{:S(2)}) collective-permute-start(bf16[1,48,1536]{2,1,0:T(8,128)(2,1)S(1)} %constant_dynamic-slice_fusion), channel_id=1, source_target_pairs={{0,8},{1,9},{2,10},{3,11},{4,12},{5,13},{6,14},{7,15},{8,0},{9,1},... | collective-permute-start | bytes 442376 | tf_op jit(solution)/shard_map/ppermute | solution.py:189
  88.0 0.2 reshape_reshape.11
  88.3 0.2 multiply_reduce_fusion
  88.5 1.3 %fusion.5 = bf16[3,192,192]{1,2,0:T(8,128)(2,1)S(1)} fusion(bf16[3,192,128]{2,1,0:T(8,128)(2,1)S(1)} %reshape.170, bf16[3,192,128]{2,1,0:T(8,128)(2,1)S(1)} %copy-done.9, f32[3,192]{1,0:T(4,128)S(1)} %multiply_reduce_fusion, f32[3,192,192]{1,2,0:T(8,128)} %get-tuple-element.28, f32[3,192]{1,0:T(4,128)S(1)} %get-tuple-element.27), kind=kOutput, calls=%fused_computation.10 | convolution fusion | flops 28753920 | bytes 963072 | tf_op jit(solution)/shard_map/dot_general | solution.py:15
  89.8 0.2 fusion.7
  90.1 0.3 fusion.6
  90.4 2.6 %collective-permute-done.3 = bf16[96,1536]{1,0:T(8,128)(2,1)S(1)} collective-permute-done((bf16[96,1536]{1,0:T(8,128)(2,1)S(1)}, bf16[96,1536]{1,0:T(8,128)(2,1)S(1)}, u32[]{:S(2)}, u32[]{:S(2)}) %collective-permute-start.3) | collective-permute-done | bytes 294944 | tf_op jit(solution)/shard_map/ppermute | solution.py:241
  93.0 0.9 convert_add_fusion.2
  93.9 1.3 %convolution_convert_fusion.2 = bf16[3,192,128]{2,1,0:T(8,128)(2,1)S(1)} fusion(bf16[3,192,128]{2,1,0:T(8,128)(2,1)S(1)} %reshape.170, f32[3,192]{1,0:T(4,128)S(1)} %get-tuple-element.27, bf16[3,192,128]{2,1,0:T(8,128)(2,1)S(1)} %copy-done.5, bf16[3,192,128]{2,1,0:T(8,128)(2,1)S(1)} %copy-done.7, pred[192,192]{0,1:T(8,128)(4,1)} %copy-done.10), kind=kOutput, calls=%fused_computation.16 | convolution fusion | flops 57250560 | bytes 628992 | tf_op jit(solution)/shard_map/dot_general | solution.py:15
  95.6 0.1 fusion.17.x_ref
  95.7 11.8 %exchange.7 = bf16[16,112,128]{2,1,0:T(8,128)(2,1)S(1)} custom-call(bf16[16,112,128]{2,1,0:T(8,128)(2,1)S(1)} %fusion.17.x_ref), custom_call_target="tpu_custom_call" | custom-call | bytes 29360128 | tf_op jit(solution)/shard_map/exchange/pallas_call | solution.py:66
  107.5 0.7 convert_add_fusion.3
  108.3 0.9 reshape_transpose_reshape.9
  109.1 0.9 reshape_transpose_reshape.10
  110.0 0.9 reshape_transpose_reshape.11
  (62 shorter events, 1.5 us)
Async XLA Ops:
  7.2 38.8 %copy-start = (bf16[96,1536]{1,0:T(8,128)(2,1)S(1)}, bf16[96,1536]{1,0:T(8,128)(2,1)}, u32[]{:S(2)}) copy-start(bf16[96,1536]{1,0:T(8,128)(2,1)} %param.10) | copy-start | bytes 884740
  7.2 58.3 %all-gather.3.cloned.1.call-start = ((), (), s32[]{:S(2)}) async-start(), calls=%async_computation | async-start | bytes 2506752 | tf_op jit(solution)/shard_map/all_gather | solution.py:151
  11.4 16.9 %copy-start.11 = (s32[1,16]{1,0:T(1,128)S(1)}, s32[1,16]{1,0:T(1,128)}, u32[]{:S(2)}) copy-start(s32[1,16]{1,0:T(1,128)} %param.11) | copy-start | bytes 196
  27.9 2.5 %copy-start.8 = (bf16[3,192,128]{2,1,0:T(8,128)(2,1)}, bf16[3,192,128]{2,1,0:T(8,128)(2,1)S(1)}, u32[]{:S(2)}) copy-start(bf16[3,192,128]{2,1,0:T(8,128)(2,1)S(1)} %reshape.162) | copy-start | bytes 442372
  28.0 1.8 %copy-start.4 = (bf16[3,192,128]{2,1,0:T(8,128)(2,1)}, bf16[3,192,128]{2,1,0:T(8,128)(2,1)S(1)}, u32[]{:S(2)}) copy-start(bf16[3,192,128]{2,1,0:T(8,128)(2,1)S(1)} %reshape.158) | copy-start | bytes 442372
  28.2 1.6 %copy-start.6 = (bf16[3,192,128]{2,1,0:T(8,128)(2,1)}, bf16[3,192,128]{2,1,0:T(8,128)(2,1)S(1)}, u32[]{:S(2)}) copy-start(bf16[3,192,128]{2,1,0:T(8,128)(2,1)S(1)} %reshape.160) | copy-start | bytes 442372
  28.6 1.9 %copy-start.10 = (pred[192,192]{0,1:T(8,128)(4,1)}, pred[192,192]{0,1:T(8,128)(4,1)S(1)}, u32[]{:S(2)}) copy-start(pred[192,192]{0,1:T(8,128)(4,1)S(1)} %compare_and_fusion) | copy-start | bytes 110596
  30.4 0.7 copy-start.2
  46.5 2.9 %collective-permute-start = (bf16[8,48,1536]{2,1,0:T(8,128)(2,1)S(1)}, bf16[8,48,1536]{2,1,0:T(8,128)(2,1)S(1)}, u32[]{:S(2)}, u32[]{:S(2)}) collective-permute-start(bf16[8,48,1536]{2,1,0:T(8,128)(2,1)S(1)} %convolution_convert_fusion), channel_id=1, source_target_pairs={{0,1},{1,0},{2,3},{3,2},{4,5},{5,4},{6,7},{7,6},{8,9},{9,8},{10,11... | collective-permute-start | bytes 3538952 | tf_op jit(solution)/shard_map/ppermute | solution.py:189
  68.0 14.4 %copy-start.1 = (bf16[16,1,48,1536]{3,2,1,0:T(8,128)(2,1)S(1)}, bf16[16,1,48,1536]{3,2,1,0:T(8,128)(2,1)}, u32[]{:S(2)}) copy-start(bf16[16,1,48,1536]{3,2,1,0:T(8,128)(2,1)} %all-gather.3.cloned.1.call-done) | copy-start | bytes 7077892
  68.7 16.3 %collective-permute-start.1 = (bf16[2,48,1536]{2,1,0:T(8,128)(2,1)}, bf16[2,48,1536]{2,1,0:T(8,128)(2,1)}, u32[]{:S(2)}, u32[]{:S(2)}) collective-permute-start(bf16[2,48,1536]{2,1,0:T(8,128)(2,1)} %dynamic-slice_bitcast_fusion.1), channel_id=1, source_target_pairs={{0,4},{1,5},{2,6},{3,7},{4,0},{5,1},{6,2},{7,3},{8,12},{9,13},{10,... | collective-permute-start | bytes 884744 | tf_op jit(solution)/shard_map/ppermute | solution.py:189
  83.9 4.4 %copy-start.3 = (bf16[3,192,128]{2,1,0:T(8,128)(2,1)S(1)}, bf16[3,192,128]{2,1,0:T(8,128)(2,1)}, u32[]{:S(2)}) copy-start(bf16[3,192,128]{2,1,0:T(8,128)(2,1)} %copy-done.2) | copy-start | bytes 442372
  83.9 4.6 %copy-start.9 = (bf16[3,192,128]{2,1,0:T(8,128)(2,1)S(1)}, bf16[3,192,128]{2,1,0:T(8,128)(2,1)}, u32[]{:S(2)}) copy-start(bf16[3,192,128]{2,1,0:T(8,128)(2,1)} %copy-done.8) | copy-start | bytes 442372
  83.9 9.1 %collective-permute-start.3 = (bf16[96,1536]{1,0:T(8,128)(2,1)S(1)}, bf16[96,1536]{1,0:T(8,128)(2,1)S(1)}, u32[]{:S(2)}, u32[]{:S(2)}) collective-permute-start(bf16[96,1536]{1,0:T(8,128)(2,1)S(1)} %convolution_convert_fusion.1), channel_id=1, source_target_pairs={{0,16},{16,0},{1,17},{17,1},{2,18},{18,2},{3,19},{19,3},{4,20},{20... | collective-permute-start | bytes 884744 | tf_op jit(solution)/shard_map/ppermute | solution.py:241
  86.1 3.7 %copy-start.5 = (bf16[3,192,128]{2,1,0:T(8,128)(2,1)S(1)}, bf16[3,192,128]{2,1,0:T(8,128)(2,1)}, u32[]{:S(2)}) copy-start(bf16[3,192,128]{2,1,0:T(8,128)(2,1)} %copy-done.4) | copy-start | bytes 442372
  86.1 21.3 %collective-permute-start.2 = (bf16[1,48,1536]{2,1,0:T(8,128)(2,1)S(1)}, bf16[1,48,1536]{2,1,0:T(8,128)(2,1)S(1)}, u32[]{:S(2)}, u32[]{:S(2)}) collective-permute-start(bf16[1,48,1536]{2,1,0:T(8,128)(2,1)S(1)} %constant_dynamic-slice_fusion), channel_id=1, source_target_pairs={{0,8},{1,9},{2,10},{3,11},{4,12},{5,13},{6,14},{7,15},{8,0},{9,1},... | collective-permute-start | bytes 442376 | tf_op jit(solution)/shard_map/ppermute | solution.py:189
  88.0 2.0 %copy-start.7 = (bf16[3,192,128]{2,1,0:T(8,128)(2,1)S(1)}, bf16[3,192,128]{2,1,0:T(8,128)(2,1)}, u32[]{:S(2)}) copy-start(bf16[3,192,128]{2,1,0:T(8,128)(2,1)} %copy-done.6) | copy-start | bytes 442372
Sparse Core Ops, SparseCore 0:
  10.3 48.5 all-gather.2
